TPU v7x, 1024 devices: a whole 4x4x32 slice. The times are simulated.
1024 devices in a mesh: task: 32 (over z), grp: 32 (over y, x, core).
Axes of the slice: x: 4, y: 4, z: 32, core: 2. Of those that a mesh axis runs over, the one named last changes fastest.
Arguments:
- amplitudes: bfloat16 [32, 640, 128], P('task'), may hold values from -6 to 6
- integrals: bfloat16 [32768, 128, 128], P(('task', 'grp')), may hold values from -0.125 to 0.125
- task_cd: int32 [32768], P(('task', 'grp')), may hold values from 0 to 31
- task_ab: int32 [32768], P(('task', 'grp')), may hold values from 0 to 63, as said below
- owner_map: int32 [64], replicated, may hold values from 0 to 63, as said below
Outputs:
- residual: float32 [640, 8192], P('task', 'grp')
Inputs may be any that keep to these rules, and one draw needn't show every extreme that they name: `task_ab`: among the tasks stored on the devices of one index of task, no two name the same pair of task_cd and residual tile. The tasks stored on one device name at most 2 residual tiles whose owner group (owner_map of the tile, divided by 2) is any one group, and on every index of task some group receives exactly 2 from every device of that index. `owner_map`: A permutation of the 64 positions; position p is owned by group p // 2.
All inputs are finite; a program needn't handle non-finite values.
Results may differ from a plain program's by a relative error of at most 0.0065.
Values may be sent and summed in bfloat16 or wider, within the bound.
No kernel may reach another device: no remote copies, remote signals or barrier semaphores. Data moves between devices by JAX's collectives and lax.ppermute only.
A program may use at most 32 MiB of HBM per device.

v0:
```python
import jax
import jax.numpy as jnp
from jax import lax
from jax.sharding import PartitionSpec as P

CAP = 2


def on_device(amplitudes, integrals, task_cd, task_ab, owner_map):
    n_grp = lax.axis_size("grp")
    n_task = lax.axis_size("task")
    width = integrals.shape[1]
    n_cd = amplitudes.shape[0] * n_task
    n_ab = owner_map.shape[0]
    ab_dev = n_ab // n_grp
    cell_count = n_cd * ab_dev
    slot_count = n_grp * CAP
    lookup = task_ab[:, None] == jnp.arange(n_ab, dtype=jnp.int32)[None, :]
    position = jnp.sum(jnp.where(lookup, owner_map[None, :], 0), axis=1)
    target = position // ab_dev
    cell_label = task_cd * ab_dev + position % ab_dev
    matches = (target[:, None] == jnp.arange(n_grp, dtype=jnp.int32)[None, :]).astype(jnp.int32)
    earlier = jnp.cumsum(matches, axis=0) - matches
    arrival = jnp.sum(matches * earlier, axis=1)
    send_slot = target * CAP + arrival
    placing = send_slot[None, :] == jnp.arange(slot_count, dtype=jnp.int32)[:, None]
    outgoing = jnp.einsum(
        "sk,kcd->scd", placing.astype(jnp.bfloat16), integrals, preferred_element_type=jnp.float32
    ).astype(jnp.bfloat16)
    labels = jnp.sum(jnp.where(placing, cell_label[None, :] + 1, 0), axis=1) - 1
    outgoing = outgoing.reshape(n_grp, CAP, width, width)
    labels = labels.reshape(n_grp, CAP)
    arrived, arrived_labels = (
        lax.all_to_all(outgoing, "grp", split_axis=0, concat_axis=0, tiled=True),
        lax.all_to_all(labels, "grp", split_axis=0, concat_axis=0, tiled=True),
    )
    flat_tiles = arrived.reshape(slot_count, width, width)
    flat_labels = arrived_labels.reshape(slot_count)
    selector = (flat_labels[None, :] == jnp.arange(cell_count, dtype=jnp.int32)[:, None]).astype(
        jnp.bfloat16
    )
    blocks = jnp.einsum(
        "ms,scd->mcd", selector, flat_tiles, preferred_element_type=jnp.float32
    ).astype(jnp.bfloat16)
    blocks = (
        blocks.reshape(n_cd, ab_dev, width, width)
        .transpose(0, 2, 1, 3)
        .reshape(n_cd, width, ab_dev * width)
    )
    partial_sum = jnp.einsum(
        "jrc,jce->re",
        lax.all_gather(amplitudes, "task", axis=0, tiled=True),
        blocks,
        preferred_element_type=jnp.float32,
    )
    return lax.psum_scatter(partial_sum, "task", scatter_dimension=0, tiled=True)


def solution(mesh):
    return jax.shard_map(
        on_device,
        mesh=mesh,
        in_specs=(
            P("task", None, None),
            P(("task", "grp"), None, None),
            P(("task", "grp")),
            P(("task", "grp")),
            P(),
        ),
        out_specs=P("task", "grp"),
        check_vma=False,
    )
```

profile of v0, /device:TPU:6, one launch (start us, length us, event | category | flops | bytes accessed | tf_op | source)
XLA Modules:
  0.0 434.8 jit_solution(15620474041734877564)
XLA Ops:
  6.5 0.0 copy-start
  6.5 0.0 all-gather.2.cloned.1.call-start
  6.5 0.7 all-gather.2.cloned.1.call-update
  7.3 0.9 select_reduce_fusion.2
  8.1 0.7 fusion.9
  8.8 0.1 fusion.5
  8.9 0.1 reduce_window_sum.11
  8.9 0.2 select_reduce_fusion.1
  9.1 0.1 select_reduce_fusion
  9.2 0.7 sub.18
  9.9 16.6 %all-to-all-start = ((s32[32,1,2]{2,1,0:T(1,128)}), s32[32,1,2]{2,1,0:T(1,128)S(1)}, u32[]{:S(2)}, u32[]{:S(2)}) async-start(s32[32,1,2]{2,1,0:T(1,128)} %bitcast), calls=%async_computation | async-start | bytes 32768 | tf_op jit(solution)/shard_map/all_to_all | solution.py:35
  26.6 0.0 copy-done
  26.6 1.0 convolution_convert_fusion.1
  27.6 3.6 copy.20
  31.2 0.9 all-to-all-done
  32.1 6.5 %all-to-all-start.1 = ((bf16[32,2,128,128]{3,1,2,0:T(2,128)(2,1)}), bf16[32,2,128,128]{3,1,2,0:T(2,128)(2,1)S(1)}, u32[]{:S(2)}, u32[]{:S(2)}) async-start(bf16[32,2,128,128]{3,1,2,0:T(2,128)(2,1)} %copy.20), calls=%async_computation.1 | async-start | bytes 4194304 | tf_op jit(solution)/shard_map/all_to_all | solution.py:34
  38.7 0.0 all-reduce.3.cloned.1.call-start
  38.7 0.5 broadcast.110
  39.2 0.7 reduce.3
  39.9 0.1 eq.65
  40.0 24.2 %all-to-all-done.1 = bf16[32,2,128,128]{3,1,2,0:T(2,128)(2,1)S(1)} async-done(((bf16[32,2,128,128]{3,1,2,0:T(2,128)(2,1)}), bf16[32,2,128,128]{3,1,2,0:T(2,128)(2,1)S(1)}, u32[]{:S(2)}, u32[]{:S(2)}) %all-to-all-start.1) | async-done | bytes 2097184 | tf_op jit(solution)/shard_map/all_to_all | solution.py:34
  64.2 2.4 copy.21
  66.6 0.7 convolution_convert_fusion
  67.3 4.1 copy.22
  71.4 93.3 %all-gather.2.cloned.1.call-done = bf16[32,640,128]{2,1,0:T(8,128)(2,1)} async-done(((bf16[1,640,128]{2,1,0:T(8,128)(2,1)}), bf16[32,640,128]{2,1,0:T(8,128)(2,1)}) %all-gather.2.cloned.1.call-update) | async-done | bytes 5242896 | tf_op jit(solution)/shard_map/all_gather | solution.py:52
  164.7 5.8 %convolution_bitcast_fusion = f32[640,256]{0,1:T(8,128)} fusion(bf16[32,128,256]{1,2,0:T(8,128)(2,1)} %bitcast.26, bf16[32,640,128]{2,1,0:T(8,128)(2,1)} %all-gather.2.cloned.1.call-done), kind=kOutput, calls=%fused_computation.2 | convolution fusion | flops 1342177280 | bytes 7995392 | tf_op jit(solution)/shard_map/jrc,jce->re/dot_general | solution.py:50
  170.5 0.0 all-reduce.3.cloned.1.call-update
  170.5 1.3 dynamic-slice
  172.4 253.7 %all-reduce.3.cloned.1.call-done = f32[640,256]{0,1:T(8,128)} async-done(((f32[640,256]{0,1:T(8,128)}), f32[640,256]{0,1:T(8,128)}) %all-reduce.3.cloned.1.call-update) | async-done | bytes 655376
  426.2 1.0 constant_dynamic-slice_fusion
  427.2 0.7 copy.23
  (2 shorter events, 0.0 us)
Async XLA Ops:
  6.5 20.0 %copy-start = (bf16[32,128,128]{2,1,0:T(8,128)(2,1)S(1)}, bf16[32,128,128]{2,1,0:T(8,128)(2,1)}, u32[]{:S(2)}) copy-start(bf16[32,128,128]{2,1,0:T(8,128)(2,1)} %param.6) | copy-start | bytes 3145732
  6.5 158.2 %all-gather.2.cloned.1.call-start = ((), (), s32[]{:S(2)}) async-start(), calls=%async_computation.2 | async-start | bytes 5406720 | tf_op jit(solution)/shard_map/all_gather | solution.py:52
  9.9 22.2 %all-to-all-start = ((s32[32,1,2]{2,1,0:T(1,128)}), s32[32,1,2]{2,1,0:T(1,128)S(1)}, u32[]{:S(2)}, u32[]{:S(2)}) async-start(s32[32,1,2]{2,1,0:T(1,128)} %bitcast), calls=%async_computation | async-start | bytes 32768 | tf_op jit(solution)/shard_map/all_to_all | solution.py:35
  32.1 32.1 %all-to-all-start.1 = ((bf16[32,2,128,128]{3,1,2,0:T(2,128)(2,1)}), bf16[32,2,128,128]{3,1,2,0:T(2,128)(2,1)S(1)}, u32[]{:S(2)}, u32[]{:S(2)}) async-start(bf16[32,2,128,128]{3,1,2,0:T(2,128)(2,1)} %copy.20), calls=%async_computation.1 | async-start | bytes 4194304 | tf_op jit(solution)/shard_map/all_to_all | solution.py:34
  38.7 387.5 %all-reduce.3.cloned.1.call-start = ((), (), s32[]{:S(2)}) async-start(), calls=%async_computation.3 | async-start | bytes 1310720
Sparse Core Ops, SparseCore 0:
  10.0 154.6 all-gather.1
  170.6 255.4 all-reduce.2
where the time goes:
time: 435 us
  waiting for transfers between devices  373 us (86%)
  starting transfers between devices  23.2 us (5%)
  local copies, waits for them, and re-layouts  14.4 us (3%)
  between operations  14.1 us (3%)
  matrix products  7.46 us (2%)
    unnamed x3, waiting for transfers between devices  254 us
    all_gather x1, waiting for transfers between devices, on_device(): lax.all_gather(amplitudes, 'task', axis=0, tiled=True)  93.3 us
    all_to_all x1, waiting for transfers between devices, on_device(): lax.all_to_all(outgoing, 'grp', split_axis=0, concat_axis=0, tiled=True)  24.2 us
    all_to_all x1, starting transfers between devices, on_device(): lax.all_to_all(labels, 'grp', split_axis=0, concat_axis=0, tiled=True)  16.6 us
  transfers between devices with their start and end apart: 4, of which 4 were waited for; matrix products, arithmetic and copies ran while one was open for 4% of the time, Pallas kernels for 0%

commit v1 on v0

v1 whole, which is shorter than its diff:
```python
import jax
import jax.numpy as jnp
from jax import lax
from jax.experimental import pallas as pl
from jax.experimental.pallas import tpu as pltpu
from jax.sharding import Mesh, PartitionSpec as P

CAP = 2
TILE = 128
ZH, ZL, NY, NX, NC = 8, 4, 4, 4, 2
Z, G = ("zh", "zl"), ("y", "x", "core")
X_ROWS, Y_ROWS = 32, 48
LABEL_ROWS = 16
MESSAGE = CAP * TILE + LABEL_ROWS
MIB = 1 << 20
SMEM = pl.BlockSpec(memory_space=pltpu.SMEM)
VMEM = pl.BlockSpec(memory_space=pltpu.VMEM)


def pack_kernel(cd_ref, ab_ref, owner_ref, tiles_ref, out_ref, count_ref, label_ref):
    groups = out_ref.shape[0]

    @pl.loop(0, groups)
    def _(g):
        count_ref[g] = 0
        for n in range(CAP):
            label_ref[CAP * g + n] = -1

    @pl.loop(0, tiles_ref.shape[0])
    def _(k):
        position = owner_ref[ab_ref[k]]
        group = position >> 1
        arrival = count_ref[group]
        count_ref[group] = arrival + 1
        label_ref[CAP * group + arrival] = 2 * cd_ref[k] + (position & 1)
        row = pl.multiple_of(arrival * TILE, TILE)
        out_ref[group, pl.ds(row, TILE), :] = tiles_ref[k]

    lane = lax.broadcasted_iota(jnp.int32, (LABEL_ROWS, TILE), 1)

    @pl.loop(0, groups)
    def _(g):
        labels = jnp.where(lane == 0, label_ref[CAP * g], label_ref[CAP * g + 1])
        out_ref[g, CAP * TILE : MESSAGE, :] = labels.astype(jnp.float32).astype(out_ref.dtype)


def pack(task_cd, task_ab, owner_map, tiles, groups):
    return pl.pallas_call(
        pack_kernel,
        out_shape=jax.ShapeDtypeStruct((groups, MESSAGE, TILE), tiles.dtype),
        in_specs=[SMEM, SMEM, SMEM, VMEM],
        out_specs=VMEM,
        scratch_shapes=[pltpu.SMEM((groups,), jnp.int32), pltpu.SMEM((groups * CAP,), jnp.int32)],
        compiler_params=pltpu.CompilerParams(vmem_limit_bytes=16 * MIB),
        cost_estimate=pl.CostEstimate(flops=0, bytes_accessed=3 * MIB, transcendentals=0),
        name="pack",
    )(task_cd, task_ab, owner_map, tiles)


def product_kernel(steps, per, place_ref, own_label, far_label, own_tiles, far_tiles, *refs):
    x_refs, (y_ref, out_ref, blocks, acc) = refs[:NX], refs[NX:]
    step = pl.program_id(0)
    core, x = place_ref[0], place_ref[1]
    width = CAP * TILE

    @pl.when(step == 0)
    def _():
        blocks[...] = jnp.zeros_like(blocks)
        acc[...] = jnp.zeros_like(acc)
        for c, (labels, tiles) in enumerate(((own_label, own_tiles), (far_label, far_tiles))):

            @pl.loop(0, tiles.shape[0])
            def _(g):
                for n in range(CAP):
                    label = labels[g, n]
                    for b in range(2):
                        column = c * width + b * TILE

                        @pl.when((label >= 0) & ((label & 1) == b))
                        def _():
                            blocks[label >> 1, :, column : column + TILE] = tiles[g, n * TILE : (n + 1) * TILE, :]

    rhs = blocks[pl.ds(step * per, per)].reshape(per * TILE, NC * width)
    lhs = jnp.concatenate(
        [
            jnp.concatenate([ref[j] for ref in x_refs] + [y_ref[y, j] for y in range(NY)], axis=0)
            for j in range(per)
        ],
        axis=1,
    )
    part = jnp.dot(lhs, rhs, preferred_element_type=jnp.float32)
    for d in range(NX):
        row = pl.multiple_of(((x - d) & (NX - 1)) * X_ROWS, X_ROWS)
        acc[pl.ds(row, X_ROWS), :] += part[d * X_ROWS : (d + 1) * X_ROWS]
    acc[NX * X_ROWS :, :] += part[NX * X_ROWS :]

    @pl.when(step == steps - 1)
    def _():
        rows = acc.shape[0] // (ZH * ZL)
        for c in range(2):
            group = core if c == 0 else 1 - core
            for z in range(ZH * ZL):
                zh, zl = z // ZL, z % ZL
                value = acc[z * rows : (z + 1) * rows, c * width : (c + 1) * width]
                out_ref[zl * NC + group, zh * rows : (zh + 1) * rows, :] = value


def product(place, own_label, far_label, own_tiles, far_tiles, along_x, along_y):
    n_cd = along_y.shape[1]
    per = 4
    steps = n_cd // per
    half = NX * X_ROWS + NY * Y_ROWS
    whole = pl.BlockSpec(own_tiles.shape, lambda i: (0, 0, 0))
    out = (ZL * NC, half // ZL, CAP * TILE)
    return pl.pallas_call(
        lambda *refs: product_kernel(steps, per, *refs),
        grid=(steps,),
        out_shape=jax.ShapeDtypeStruct(out, jnp.float32),
        in_specs=[SMEM, SMEM, SMEM, whole, whole]
        + [pl.BlockSpec((per, X_ROWS, TILE), lambda i: (i, 0, 0))] * NX
        + [pl.BlockSpec((NY, per, Y_ROWS, TILE), lambda i: (0, i, 0, 0))],
        out_specs=pl.BlockSpec(out, lambda i: (0, 0, 0)),
        scratch_shapes=[
            pltpu.VMEM((n_cd, TILE, NC * CAP * TILE), jnp.bfloat16),
            pltpu.VMEM((half, NC * CAP * TILE), jnp.float32),
        ],
        compiler_params=pltpu.CompilerParams(vmem_limit_bytes=32 * MIB),
        cost_estimate=pl.CostEstimate(
            flops=2 * half * n_cd * TILE * NC * CAP * TILE, bytes_accessed=8 * MIB, transcendentals=0
        ),
        name="product",
    )(place, own_label, far_label, own_tiles, far_tiles, *along_x, along_y)


def near_kernel(in_ref, out_ref):
    rows = in_ref.shape[1] // ZH
    for c in range(NC):
        total = in_ref[c]
        for zl in range(1, ZL):
            total = total + in_ref[zl * NC + c]
        for zh in range(ZH):
            for b in range(2):
                row = (b * NC + c) * rows
                out_ref[zh, row : row + rows, :] = total[zh * rows : (zh + 1) * rows, b * TILE : (b + 1) * TILE]


def far_kernel(in_ref, out_ref):
    total = in_ref[0]
    for zh in range(1, ZH):
        total = total + in_ref[zh]
    rows = total.shape[0] // 2
    for b in range(2):
        out_ref[:, b * TILE : (b + 1) * TILE] = total[b * rows : (b + 1) * rows]


def local_sum(kernel, value, shape, name):
    return pl.pallas_call(
        kernel,
        out_shape=jax.ShapeDtypeStruct(shape, jnp.float32),
        in_specs=[VMEM],
        out_specs=VMEM,
        cost_estimate=pl.CostEstimate(flops=value.size, bytes_accessed=4 * value.size, transcendentals=0),
        name=name,
    )(value)


def on_device(amplitudes, integrals, task_cd, task_ab, owner_map):
    groups = lax.axis_size(G)
    core, x, y = (lax.axis_index(a) for a in ("core", "x", "y"))
    rows = amplitudes.shape[1] // (ZH * ZL)
    half = NX * X_ROWS + NY * Y_ROWS
    with jax.named_scope("pack"):
        share = amplitudes.reshape(ZH * ZL, NC, rows // NC, TILE)
        share = lax.dynamic_index_in_dim(share, core, 1, keepdims=False).reshape(half, TILE)
        share = jnp.concatenate(
            [
                lax.dynamic_slice_in_dim(share, x * X_ROWS, X_ROWS, 0),
                lax.dynamic_slice_in_dim(share, NX * X_ROWS + y * Y_ROWS, Y_ROWS, 0),
            ]
        )[None]
        outgoing = pack(task_cd, task_ab, owner_map, integrals, groups)
        outgoing, share = lax.optimization_barrier((outgoing, share))
    with jax.named_scope("route_tiles"):
        own_tiles = lax.all_to_all(outgoing, G, 0, 0, tiled=True)
    with jax.named_scope("gather_amplitudes"):
        gathered = lax.all_gather(share, Z, axis=0, tiled=True)
        part_x, part_y = gathered[:, :X_ROWS], gathered[:, X_ROWS:]
        along_y = lax.all_to_all(jnp.broadcast_to(part_y, (NY, *part_y.shape)), "y", 0, 0, tiled=True)
        along_x = [part_x] + [
            lax.ppermute(part_x, "x", [(i, (i + d) % NX) for i in range(NX)]) for d in range(1, NX)
        ]
    with jax.named_scope("share_tiles"):
        own_tiles, _ = lax.optimization_barrier((own_tiles, part_x))
        far_tiles = lax.ppermute(own_tiles, "core", [(0, 1), (1, 0)])
        own_label, far_label = (t[:, CAP * TILE, :CAP].astype(jnp.int32) for t in (own_tiles, far_tiles))
    with jax.named_scope("product"):
        partial = product(jnp.stack([core, x]), own_label, far_label, own_tiles, far_tiles, along_x, along_y)
    with jax.named_scope("reduce"):
        near = lax.all_to_all(partial, ("zl", "core"), 0, 0, tiled=True)
        near = local_sum(near_kernel, near, (ZH, 2 * rows, TILE), "near_sum")
        far = lax.all_to_all(near, "zh", 0, 0, tiled=True)
        return local_sum(far_kernel, far, (rows, CAP * TILE), "far_sum")


def solution(mesh):
    split = Mesh(mesh.devices.reshape(ZH, ZL, NY, NX, NC), Z + G)
    return jax.shard_map(
        on_device,
        mesh=split,
        in_specs=(P(Z), P(Z + G), P(Z + G), P(Z + G), P()),
        out_specs=P(Z, G),
        check_vma=False,
    )
```

time: 435 us -> 195 us (0.45)
  waiting for transfers between devices: 373 us -> 10.8 us
  blocking collectives: 0 us -> 127 us
  Pallas kernels: 0 us -> 14.3 us
  between operations: 14.1 us -> 0.16 us
  starting transfers between devices: 23.2 us -> 33.1 us
  matrix products: 7.46 us -> 0 us
  local copies, waits for them, and re-layouts: 14.4 us -> 7 us
    unnamed x3 -> x0, waiting for transfers between devices: 254 us -> none
    all_gather x1 -> x0, waiting for transfers between devices: 93.3 us -> none  [on_device(): lax.all_gather(amplitudes, 'task', axis=0, tiled=True)]
    all_to_all x0 -> x2, blocking collectives: none -> 64.9 us  [the longest x1 43.6 us: on_device(): far = lax.all_to_all(near, 'zh', 0, 0, tiled=True)]
    all_gather x0 -> x1, blocking collectives: none -> 62.1 us  [on_device(): gathered = lax.all_gather(share, Z, axis=0, tiled=True)]
    all_to_all x2, waiting for transfers between devices: 25.1 us -> 1.72 us  [the longest x1 1.72 us: on_device(): lax.all_to_all(jnp.broadcast_to(part_y, (NY, *part_y.shape)), 'y', 0, 0,...]
    pallas_call x0 -> x4, Pallas kernels: none -> 14.3 us  [the longest x1 9.44 us: product(): pl.pallas_call(lambda *refs: product_kernel(steps, per, *refs), grid=(ste...]
    ppermute x0 -> x4, starting transfers between devices: none -> 11.7 us  [the longest x3 9.8 us: on_device(): lax.ppermute(part_x, 'x', [(i, (i + d) % NX) for i in range(NX)])]
    ppermute x0 -> x4, waiting for transfers between devices: none -> 9.1 us  [the longest x3 9.1 us: on_device(): lax.ppermute(part_x, 'x', [(i, (i + d) % NX) for i in range(NX)])]
  transfers between devices with their start and end apart: 4 -> 6, of which waited for: 4 -> 3; matrix products, arithmetic and copies ran while one was open for 4% -> 1% of each run, Pallas kernels for 0% -> 0%
where the time goes in v1:
time: 195 us; the launch traced here: 193 us
  blocking collectives  127 us (65%)
  starting transfers between devices  33.1 us (17%)
  Pallas kernels  14.3 us (7%)
  waiting for transfers between devices  10.8 us (6%)
  local copies, waits for them, and re-layouts  7 us (4%)
    all_gather x1, blocking collectives, on_device(): gathered = lax.all_gather(share, Z, axis=0, tiled=True)  62.1 us
    all_to_all x1, blocking collectives, on_device(): far = lax.all_to_all(near, 'zh', 0, 0, tiled=True)  43.6 us
    all_to_all x1, blocking collectives, on_device(): near = lax.all_to_all(partial, ('zl', 'core'), 0, 0, tiled=True)  21.3 us
    all_to_all x1, starting transfers between devices, on_device(): own_tiles = lax.all_to_all(outgoing, G, 0, 0, tiled=True)  16.9 us
    ppermute x3, starting transfers between devices, on_device(): lax.ppermute(part_x, 'x', [(i, (i + d) % NX) for i in range(NX)])  9.8 us
    pallas_call x1, Pallas kernels, product(): pl.pallas_call(lambda *refs: product_kernel(steps, per, *refs), grid=(ste...  9.44 us
    ppermute x3, waiting for transfers between devices, on_device(): lax.ppermute(part_x, 'x', [(i, (i + d) % NX) for i in range(NX)])  9.1 us
    unnamed x10, local copies, waits for them, and re-layouts  4.55 us
  transfers between devices with their start and end apart: 6, of which 3 were waited for; matrix products, arithmetic and copies ran while one was open for 1% of the time, Pallas kernels for 0%

profile of v1, /device:TPU:6, one launch (start us, length us, event | category | flops | bytes accessed | tf_op | source)
XLA Modules:
  0.0 193.3 jit_solution(7921723361579950431)
XLA Ops:
  0.0 1.0 reshape.11
  1.1 0.0 copy-start.1
  1.1 1.2 copy-done.1
  2.3 0.0 copy-start.2
  2.3 0.7 copy-done.2
  3.0 0.0 copy-start.3
  3.0 0.7 copy-done.3
  3.6 0.0 copy-start.4
  3.6 0.7 copy-done.4
  4.3 1.5 pack.1
  5.8 0.0 copy-start
  5.8 1.4 copy-done
  7.2 16.9 %all-to-all-start = ((bf16[32,272,128]{2,1,0:T(8,128)(2,1)}), bf16[32,272,128]{2,1,0:T(8,128)(2,1)S(1)}, u32[]{:S(2)}, u32[]{:S(2)}) async-start(bf16[32,272,128]{2,1,0:T(8,128)(2,1)} %copy-done), calls=%async_computation | async-start | bytes 4456448 | tf_op jit(solution)/shard_map/route_tiles/all_to_all | solution.py:184
  24.1 62.1 %all_gather.3 = bf16[32,80,128]{2,1,0:T(8,128)(2,1)S(1)} all-gather(bf16[1,80,128]{2,1,0:T(8,128)(2,1)S(1)} %maximum_bitcast_fusion), channel_id=1, replica_groups=mesh['zh'=8,'zl'=4,'y'=4,'x'=4,'core'=2] {'zh','zl'}, dimensions={0}, use_global_device_ids=true | all-gather | bytes 675840 | tf_op jit(solution)/shard_map/gather_amplitudes/all_gather | solution.py:186
  86.2 0.0 all-to-all-done.refs_3_
  86.2 1.9 collective-permute-start
  88.2 1.4 broadcast_in_dim.7
  89.5 4.5 %all-to-all-start.1 = ((bf16[4,32,48,128]{3,2,1,0:T(8,128)(2,1)}), bf16[4,32,48,128]{3,2,1,0:T(8,128)(2,1)}, u32[]{:S(2)}, u32[]{:S(2)}) async-start(bf16[4,32,48,128]{3,2,1,0:T(8,128)(2,1)} %broadcast_in_dim.7), calls=%async_computation.1 | async-start | bytes 3145728 | tf_op jit(solution)/shard_map/gather_amplitudes/all_to_all | solution.py:188
  94.0 2.7 %collective-permute-start.3 = (bf16[32,32,128]{2,1,0:T(8,128)(2,1)S(1)}, bf16[32,32,128]{2,1,0:T(8,128)(2,1)S(1)}, u32[]{:S(2)}, u32[]{:S(2)}) collective-permute-start(bf16[32,32,128]{2,1,0:T(8,128)(2,1)S(1)} %slice.16.refs_5_), channel_id=1, source_target_pairs={{0,6},{2,0},{4,2},{6,4},{1,7},{3,1},{5,3},{7,5},{8,14},{10,8},{12,... | collective-permute-start | bytes 786440 | tf_op jit(solution)/shard_map/gather_amplitudes/ppermute | solution.py:190
  96.7 3.0 %collective-permute-start.2 = (bf16[32,32,128]{2,1,0:T(8,128)(2,1)S(1)}, bf16[32,32,128]{2,1,0:T(8,128)(2,1)S(1)}, u32[]{:S(2)}, u32[]{:S(2)}) collective-permute-start(bf16[32,32,128]{2,1,0:T(8,128)(2,1)S(1)} %slice.16.refs_5_), channel_id=1, source_target_pairs={{0,4},{2,6},{4,0},{6,2},{1,5},{3,7},{5,1},{7,3},{8,12},{10,14},{12... | collective-permute-start | bytes 786440 | tf_op jit(solution)/shard_map/gather_amplitudes/ppermute | solution.py:190
  99.7 4.1 %collective-permute-start.1 = (bf16[32,32,128]{2,1,0:T(8,128)(2,1)S(1)}, bf16[32,32,128]{2,1,0:T(8,128)(2,1)S(1)}, u32[]{:S(2)}, u32[]{:S(2)}) collective-permute-start(bf16[32,32,128]{2,1,0:T(8,128)(2,1)S(1)} %slice.16.refs_5_), channel_id=1, source_target_pairs={{0,2},{2,4},{4,6},{6,0},{1,3},{3,5},{5,7},{7,1},{8,10},{10,12},{12... | collective-permute-start | bytes 786440 | tf_op jit(solution)/shard_map/gather_amplitudes/ppermute | solution.py:190
  103.8 0.1 pad_add_fusion.refs_0_
  103.9 0.0 collective-permute-done.refs_4_
  103.9 0.9 slice_convert_fusion
  104.8 6.6 %collective-permute-done.3.refs_8_ = bf16[32,32,128]{2,1,0:T(8,128)(2,1)S(1)} collective-permute-done((bf16[32,32,128]{2,1,0:T(8,128)(2,1)S(1)}, bf16[32,32,128]{2,1,0:T(8,128)(2,1)S(1)}, u32[]{:S(2)}, u32[]{:S(2)}) %collective-permute-start.3) | collective-permute-done | bytes 262176 | tf_op jit(solution)/shard_map/gather_amplitudes/ppermute | solution.py:190
  111.4 0.0 collective-permute-done.2.refs_7_
  111.4 2.5 %collective-permute-done.1.refs_6_ = bf16[32,32,128]{2,1,0:T(8,128)(2,1)S(1)} collective-permute-done((bf16[32,32,128]{2,1,0:T(8,128)(2,1)S(1)}, bf16[32,32,128]{2,1,0:T(8,128)(2,1)S(1)}, u32[]{:S(2)}, u32[]{:S(2)}) %collective-permute-start.1) | collective-permute-done | bytes 262176 | tf_op jit(solution)/shard_map/gather_amplitudes/ppermute | solution.py:190
  113.9 1.7 all-to-all-done.1.refs_9_
  115.6 9.4 %product.1 = f32[8,80,256]{2,1,0:T(8,128)S(1)} custom-call(s32[2]{0:T(128)S(1)} %pad_add_fusion.refs_0_, s32[32,2]{1,0:T(8,128)S(1)} %bitcast.6, s32[32,2]{1,0:T(8,128)S(1)} %bitcast.7, bf16[32,272,128]{2,1,0:T(8,128)(2,1)S(1)} %all-to-all-done.refs_3_, bf16[32,272,128]{2,1,0:T(8,128)(2,1)} %collective-permute-done.refs_4_, ...), custom_call_target="tpu_custom_call" | custom-call | flops 1342177280 | bytes 8388608 | tf_op jit(solution)/shard_map/product/product/pallas_call | solution.py:115
  125.1 21.3 %all_to_all.20.in_ref = f32[8,80,256]{2,1,0:T(8,128)} all-to-all(f32[8,80,256]{2,1,0:T(8,128)S(1)} %product.1), channel_id=1, replica_groups=mesh['zh'=8,'zl'=4,'y'=4,'x'=4,'core'=2] {'zl','core'}, dimensions={0} | all-to-all | bytes 1310720 | tf_op jit(solution)/shard_map/reduce/all_to_all | solution.py:199
  146.3 1.8 near_sum.1
  148.1 43.6 %all_to_all.21.in_ref = f32[8,40,128]{2,1,0:T(8,128)} all-to-all(f32[8,40,128]{2,1,0:T(8,128)} %near_sum.1), channel_id=1, replica_groups=mesh['zh'=8,'zl'=4,'y'=4,'x'=4,'core'=2] {'zh'}, dimensions={0} | all-to-all | bytes 327680 | tf_op jit(solution)/shard_map/reduce/all_to_all | solution.py:201
  191.8 1.5 far_sum.1
  (8 shorter events, 0.1 us)
Async XLA Ops:
  1.1 1.2 copy-start.1
  2.3 0.7 copy-start.2
  3.0 0.7 copy-start.3
  3.6 0.7 copy-start.4
  5.8 1.4 copy-start
  7.2 79.0 %all-to-all-start = ((bf16[32,272,128]{2,1,0:T(8,128)(2,1)}), bf16[32,272,128]{2,1,0:T(8,128)(2,1)S(1)}, u32[]{:S(2)}, u32[]{:S(2)}) async-start(bf16[32,272,128]{2,1,0:T(8,128)(2,1)} %copy-done), calls=%async_computation | async-start | bytes 4456448 | tf_op jit(solution)/shard_map/route_tiles/all_to_all | solution.py:184
  86.2 17.7 %collective-permute-start = (bf16[32,272,128]{2,1,0:T(8,128)(2,1)S(1)}, bf16[32,272,128]{2,1,0:T(8,128)(2,1)}, u32[]{:S(2)}, u32[]{:S(2)}) collective-permute-start(bf16[32,272,128]{2,1,0:T(8,128)(2,1)S(1)} %all-to-all-done.refs_3_), channel_id=1, source_target_pairs={{0,1},{1,0},{2,3},{3,2},{4,5},{5,4},{6,7},{7,6},{8,9},{9,8},{10,11... | collective-permute-start | bytes 6684680 | tf_op jit(solution)/shard_map/share_tiles/ppermute | solution.py:194
  89.5 26.1 %all-to-all-start.1 = ((bf16[4,32,48,128]{3,2,1,0:T(8,128)(2,1)}), bf16[4,32,48,128]{3,2,1,0:T(8,128)(2,1)}, u32[]{:S(2)}, u32[]{:S(2)}) async-start(bf16[4,32,48,128]{3,2,1,0:T(8,128)(2,1)} %broadcast_in_dim.7), calls=%async_computation.1 | async-start | bytes 3145728 | tf_op jit(solution)/shard_map/gather_amplitudes/all_to_all | solution.py:188
  94.0 17.4 %collective-permute-start.3 = (bf16[32,32,128]{2,1,0:T(8,128)(2,1)S(1)}, bf16[32,32,128]{2,1,0:T(8,128)(2,1)S(1)}, u32[]{:S(2)}, u32[]{:S(2)}) collective-permute-start(bf16[32,32,128]{2,1,0:T(8,128)(2,1)S(1)} %slice.16.refs_5_), channel_id=1, source_target_pairs={{0,6},{2,0},{4,2},{6,4},{1,7},{3,1},{5,3},{7,5},{8,14},{10,8},{12,... | collective-permute-start | bytes 786440 | tf_op jit(solution)/shard_map/gather_amplitudes/ppermute | solution.py:190
  96.7 14.7 %collective-permute-start.2 = (bf16[32,32,128]{2,1,0:T(8,128)(2,1)S(1)}, bf16[32,32,128]{2,1,0:T(8,128)(2,1)S(1)}, u32[]{:S(2)}, u32[]{:S(2)}) collective-permute-start(bf16[32,32,128]{2,1,0:T(8,128)(2,1)S(1)} %slice.16.refs_5_), channel_id=1, source_target_pairs={{0,4},{2,6},{4,0},{6,2},{1,5},{3,7},{5,1},{7,3},{8,12},{10,14},{12... | collective-permute-start | bytes 786440 | tf_op jit(solution)/shard_map/gather_amplitudes/ppermute | solution.py:190
  99.7 14.2 %collective-permute-start.1 = (bf16[32,32,128]{2,1,0:T(8,128)(2,1)S(1)}, bf16[32,32,128]{2,1,0:T(8,128)(2,1)S(1)}, u32[]{:S(2)}, u32[]{:S(2)}) collective-permute-start(bf16[32,32,128]{2,1,0:T(8,128)(2,1)S(1)} %slice.16.refs_5_), channel_id=1, source_target_pairs={{0,2},{2,4},{4,6},{6,0},{1,3},{3,5},{5,7},{7,1},{8,10},{10,12},{12... | collective-permute-start | bytes 786440 | tf_op jit(solution)/shard_map/gather_amplitudes/ppermute | solution.py:190

commit v2 on v1

v2 whole, which is shorter than its diff:
```python
import jax
import jax.numpy as jnp
from jax import lax
from jax.experimental import pallas as pl
from jax.experimental.pallas import tpu as pltpu
from jax.sharding import Mesh, PartitionSpec as P

CAP = 2
TILE = 128
ZH, ZL, NY, NX, NC = 8, 4, 4, 4, 2
Z, G = ("zh", "zl"), ("y", "x", "core")
PIECES = 4
LABEL_ROWS = 16
MESSAGE = CAP * TILE + LABEL_ROWS
MIB = 1 << 20
PER = 8
MARGIN = 16
TOP = 14
TINY = 1e-30
SMEM = pl.BlockSpec(memory_space=pltpu.SMEM)
VMEM = pl.BlockSpec(memory_space=pltpu.VMEM)


def pack_kernel(
    cd_ref, ab_ref, owner_ref, tiles_ref, out_ref, count_ref, label_ref, task_ref, held, message, in_sem, out_sems
):
    tasks, groups, parts = tiles_ref.shape[0], out_ref.shape[0], out_sems.shape[0]
    fetch = pltpu.make_async_copy(tiles_ref, held, in_sem)
    fetch.start()

    @pl.loop(0, groups)
    def _(g):
        count_ref[g] = 0
        for n in range(CAP):
            label_ref[CAP * g + n] = -1

    @pl.loop(0, tasks)
    def _(k):
        position = owner_ref[ab_ref[k]]
        group = position >> 1
        arrival = count_ref[group]
        count_ref[group] = arrival + 1
        cd = cd_ref[k]
        cell = (cd & (ZL - 1)) * ZH + (cd >> 2)
        label_ref[CAP * group + arrival] = 2 * cell + (position & 1)
        task_ref[CAP * group + arrival] = k

    fetch.wait()
    lane = lax.broadcasted_iota(jnp.int32, (LABEL_ROWS, TILE), 1)
    size = groups // parts
    sends = []
    for part in range(parts):

        @pl.loop(part * size, (part + 1) * size)
        def _(g):
            for n in range(CAP):

                @pl.when(label_ref[CAP * g + n] >= 0)
                def _():
                    message[g, n * TILE : (n + 1) * TILE, :] = held[task_ref[CAP * g + n]]

            labels = jnp.where(lane == 0, label_ref[CAP * g], label_ref[CAP * g + 1])
            message[g, CAP * TILE :, :] = labels.astype(jnp.float32).astype(message.dtype)

        group = pl.ds(part * size, size)
        sends.append(pltpu.make_async_copy(message.at[group], out_ref.at[group], out_sems.at[part]))
        sends[-1].start()
    for send in sends:
        send.wait()


def pack(task_cd, task_ab, owner_map, tiles, groups):
    out = (groups, MESSAGE, TILE)
    return pl.pallas_call(
        pack_kernel,
        out_shape=jax.ShapeDtypeStruct(out, tiles.dtype),
        in_specs=[SMEM, SMEM, SMEM, pl.BlockSpec(memory_space=pl.ANY)],
        out_specs=pl.BlockSpec(memory_space=pl.ANY),
        scratch_shapes=[
            pltpu.SMEM((groups,), jnp.int32),
            pltpu.SMEM((groups * CAP,), jnp.int32),
            pltpu.SMEM((groups * CAP,), jnp.int32),
            pltpu.VMEM(tiles.shape, tiles.dtype),
            pltpu.VMEM(out, tiles.dtype),
            pltpu.SemaphoreType.DMA,
            pltpu.SemaphoreType.DMA((4,)),
        ],
        compiler_params=pltpu.CompilerParams(vmem_limit_bytes=56 * MIB),
        cost_estimate=pl.CostEstimate(flops=0, bytes_accessed=3 * MIB, transcendentals=0),
        name="pack",
    )(task_cd, task_ab, owner_map, tiles)


def cells_kernel(own_label, far_label, own_tiles, far_tiles, out_ref):
    out_ref[...] = jnp.zeros_like(out_ref)
    for c, (labels, tiles) in enumerate(((own_label, own_tiles), (far_label, far_tiles))):

        @pl.loop(0, tiles.shape[0])
        def _(g):
            for n in range(CAP):
                label = labels[g, n]
                for b in range(2):
                    column = (c * CAP + b) * TILE

                    @pl.when((label >= 0) & ((label & 1) == b))
                    def _():
                        out_ref[label >> 1, :, column : column + TILE] = tiles[g, n * TILE : (n + 1) * TILE, :]


def cells(own_label, far_label, own_tiles, far_tiles, n_cd):
    return pl.pallas_call(
        cells_kernel,
        out_shape=jax.ShapeDtypeStruct((n_cd, TILE, NC * CAP * TILE), own_tiles.dtype),
        in_specs=[SMEM, SMEM, VMEM, VMEM],
        out_specs=VMEM,
        compiler_params=pltpu.CompilerParams(vmem_limit_bytes=16 * MIB),
        cost_estimate=pl.CostEstimate(flops=0, bytes_accessed=12 * MIB, transcendentals=0),
        name="cells",
    )(own_label, far_label, own_tiles, far_tiles)


def product_kernel(place_ref, cells_ref, *refs):
    pieces, (out_ref, sorted_rows) = refs[:PIECES], refs[PIECES:]
    core, place = place_ref[0], place_ref[1]
    width = CAP * TILE
    size = pieces[0].shape[1]
    acc = None
    for i in range(0, cells_ref.shape[0], PER):
        lhs = jnp.concatenate(
            [jnp.concatenate([piece[j] for piece in pieces], axis=0) for j in range(i, i + PER)], axis=1
        )
        rhs = cells_ref[i : i + PER].reshape(PER * TILE, NC * width)
        part = jnp.dot(lhs, rhs, preferred_element_type=jnp.float32)
        acc = part if acc is None else acc + part
    peak = jnp.maximum(jnp.max(jnp.abs(acc)), TINY)
    power = jnp.ceil(jnp.log2(jnp.full((MARGIN, width), peak, jnp.float32)))
    scale = jnp.exp2(TOP - power)[:1, :1]
    for d in range(PIECES):
        row = pl.multiple_of(((place - d) & (PIECES - 1)) * size, size)
        sorted_rows[pl.ds(row, size), :] = acc[d * size : (d + 1) * size] * scale
    block = acc.shape[0] // ZL
    rows = 2 * block // ZH
    for c in range(NC):
        group = core if c == 0 else 1 - core
        for zl in range(ZL):
            for h in range(ZH // NC):
                z = h * ZL + zl
                value = sorted_rows[z * rows : (z + 1) * rows, c * width : (c + 1) * width]
                out_ref[zl * NC + group, h * rows : (h + 1) * rows, :] = value
            out_ref[zl * NC + group, block:, :] = power


def product(place, filled, pieces):
    half = PIECES * pieces[0].shape[1]
    out = (ZL * NC, half // ZL + MARGIN, CAP * TILE)
    return pl.pallas_call(
        product_kernel,
        out_shape=jax.ShapeDtypeStruct(out, jnp.float32),
        in_specs=[SMEM] + [VMEM] * (1 + PIECES),
        out_specs=VMEM,
        scratch_shapes=[pltpu.VMEM((half, NC * CAP * TILE), jnp.float32)],
        compiler_params=pltpu.CompilerParams(vmem_limit_bytes=16 * MIB),
        cost_estimate=pl.CostEstimate(
            flops=2 * half * filled.size, bytes_accessed=8 * MIB, transcendentals=0
        ),
        name="product",
    )(place, filled, *pieces)


def near_kernel(in_ref, out_ref):
    block = in_ref.shape[1] - MARGIN
    rows = NC * block // ZH
    power = in_ref[0, block : block + 8, :]
    for s in range(1, ZL * NC):
        power = jnp.maximum(power, in_ref[s, block : block + 8, :])
    power = power + 2
    for c in range(NC):
        total = None
        for zl in range(ZL):
            s = zl * NC + c
            scale = jnp.exp2(in_ref[s, block : block + 8, :] - power)[:1]
            term = in_ref[s, :block, :] * scale
            total = term if total is None else total + term
        for h in range(ZH // NC):
            zh = c * (ZH // NC) + h
            out_ref[zh, :rows, :] = total[h * rows : (h + 1) * rows]
            out_ref[zh, rows:, :] = power[: out_ref.shape[1] - rows]


def far_kernel(in_ref, out_ref):
    rows = out_ref.shape[0]
    total = None
    for zh in range(ZH):
        term = in_ref[zh, :rows, :] * jnp.exp2(in_ref[zh, rows : rows + 1, :] - TOP)
        total = term if total is None else total + term
    out_ref[...] = total


def local_sum(kernel, value, shape, name):
    return pl.pallas_call(
        kernel,
        out_shape=jax.ShapeDtypeStruct(shape, jnp.float32),
        in_specs=[VMEM],
        out_specs=VMEM,
        cost_estimate=pl.CostEstimate(flops=value.size, bytes_accessed=4 * value.size, transcendentals=0),
        name=name,
    )(value)


def narrow_all_to_all(value, axes):
    sent = lax.all_to_all(value.astype(jnp.float16), axes, 0, 0, tiled=True)
    return sent.astype(jnp.float32)


def step(d):
    pairs = []
    for y in range(NY):
        for x in range(NX):
            for core, (to_y, to_x) in enumerate(((y, (x + d) % NX), ((y + d) % NY, x))):
                pairs.append(((y * NX + x) * NC + core, (to_y * NX + to_x) * NC + core))
    return pairs


def on_device(amplitudes, integrals, task_cd, task_ab, owner_map):
    groups = lax.axis_size(G)
    core, x, y = (lax.axis_index(a) for a in ("core", "x", "y"))
    rows = amplitudes.shape[1] // (ZH * ZL)
    half = amplitudes.shape[1] // NC
    place = jnp.where(core == 0, x, y)
    with jax.named_scope("pack"):
        size = half // PIECES
        share = lax.dynamic_slice_in_dim(amplitudes, core * half + place * size, size, 1)
        outgoing = pack(task_cd, task_ab, owner_map, integrals, groups)
        outgoing, share = lax.optimization_barrier((outgoing, share))
    with jax.named_scope("route_tiles"):
        own_tiles = lax.all_to_all(outgoing, G, 0, 0, tiled=True)
    with jax.named_scope("gather_amplitudes"):
        gathered = lax.all_gather(lax.all_gather(share, "zh", axis=0, tiled=True), "zl", axis=0, tiled=True)
        pieces = [gathered] + [lax.ppermute(gathered, G, step(d)) for d in range(1, PIECES)]
    with jax.named_scope("share_tiles"):
        own_tiles, _ = lax.optimization_barrier((own_tiles, gathered))
        far_tiles = lax.ppermute(own_tiles, "core", [(0, 1), (1, 0)])
        own_label, far_label = (t[:, CAP * TILE, :CAP].astype(jnp.int32) for t in (own_tiles, far_tiles))
    with jax.named_scope("product"):
        filled = cells(own_label, far_label, own_tiles, far_tiles, ZH * ZL)
        partial = product(jnp.stack([core, place]), filled, pieces)
    with jax.named_scope("reduce"):
        near = narrow_all_to_all(partial, ("zl", "core"))
        near = local_sum(near_kernel, near, (ZH, rows + 4, CAP * TILE), "near_sum")
        far = narrow_all_to_all(near, "zh")
        return local_sum(far_kernel, far, (rows, CAP * TILE), "far_sum")


def solution(mesh):
    split = Mesh(mesh.devices.reshape(ZH, ZL, NY, NX, NC), Z + G)
    return jax.shard_map(
        on_device,
        mesh=split,
        in_specs=(P(Z), P(Z + G), P(Z + G), P(Z + G), P()),
        out_specs=P(Z, G),
        check_vma=False,
    )
```

time: 195 us -> 170 us (0.87)
  blocking collectives: 127 us -> 114 us
  local copies, waits for them, and re-layouts: 7 us -> 0.92 us
  starting transfers between devices: 33.1 us -> 27.3 us
    all_to_all x2, blocking collectives: 64.9 us -> 54 us  [narrow_all_to_all(): sent = lax.all_to_all(value.astype(jnp.float16), axes, 0, 0, tiled=True)]
    all_to_all x1 -> x0, starting transfers between devices: 4.47 us -> none  [on_device(): lax.all_to_all(jnp.broadcast_to(part_y, (NY, *part_y.shape)), 'y', 0, 0,...]
    unnamed x10 -> x2, local copies, waits for them, and re-layouts: 4.55 us -> 0.92 us
    convert_element_type x0 -> x4, other arithmetic: none -> 2.65 us  [the longest x2 1.64 us: narrow_all_to_all(): return sent.astype(jnp.float32)]
    all_gather x1 -> x2, blocking collectives: 62.1 us -> 60 us  [the longest x1 43.4 us: on_device(): lax.all_gather(share, 'zh', axis=0, tiled=True)]
    pallas_call x2 -> x3, Pallas kernels: 11 us -> 9.8 us  [the longest x1 3.89 us: cells(): pl.pallas_call(cells_kernel, out_shape=jax.ShapeDtypeStruct((n_cd, TILE,...]
  transfers between devices with their start and end apart: 6 -> 5, of which waited for: 3 -> 2; matrix products, arithmetic and copies ran while one was open for 1% -> 0% of each run, Pallas kernels for 0% -> 2%
where the time goes in v2:
time: 170 us; the launch traced here: 169 us
  blocking collectives  114 us (67%)
  starting transfers between devices  27.3 us (16%)
  Pallas kernels  13.2 us (8%)
  waiting for transfers between devices  10.6 us (6%)
  other arithmetic  2.76 us (2%)
    all_to_all x2, blocking collectives, narrow_all_to_all(): sent = lax.all_to_all(value.astype(jnp.float16), axes, 0, 0, tiled=True)  54 us
    all_gather x1, blocking collectives, on_device(): lax.all_gather(share, 'zh', axis=0, tiled=True)  43.4 us
    all_to_all x1, starting transfers between devices, on_device(): own_tiles = lax.all_to_all(outgoing, G, 0, 0, tiled=True)  16.9 us
    all_gather x1, blocking collectives, on_device(): lax.all_gather(lax.all_gather(share, 'zh', axis=0, tiled=True), 'zl', axi...  16.6 us
    ppermute x3, waiting for transfers between devices, on_device(): lax.ppermute(gathered, G, step(d))  10.6 us
    ppermute x3, starting transfers between devices, on_device(): lax.ppermute(gathered, G, step(d))  8.49 us
    pallas_call x1, Pallas kernels, cells(): pl.pallas_call(cells_kernel, out_shape=jax.ShapeDtypeStruct((n_cd, TILE,...  3.89 us
    pallas_call x1, Pallas kernels, pack(): pl.pallas_call(pack_kernel, out_shape=jax.ShapeDtypeStruct(out, tiles.dty...  3.62 us
  transfers between devices with their start and end apart: 5, of which 2 were waited for; matrix products, arithmetic and copies ran while one was open for 0% of the time, Pallas kernels for 2%

profile of v2, /device:TPU:6, one launch (start us, length us, event | category | flops | bytes accessed | tf_op | source)
XLA Modules:
  0.0 168.9 jit_solution(10988827570339974571)
XLA Ops:
  0.0 0.0 copy-start
  0.0 0.9 copy-done
  0.9 3.6 %pack.1 = bf16[32,272,128]{2,1,0:T(8,128)(2,1)} custom-call(s32[32]{0:T(128)} %cd_ref.1, s32[32]{0:T(128)} %ab_ref.1, s32[64]{0:T(128)} %owner_ref.1, bf16[32,128,128]{2,1,0:T(8,128)(2,1)} %tiles_ref.1), custom_call_target="tpu_custom_call" | custom-call | bytes 3145728 | tf_op jit(solution)/shard_map/pack/pack/pallas_call | solution.py:74
  4.5 16.9 %all-to-all-start = ((bf16[32,272,128]{2,1,0:T(8,128)(2,1)}), bf16[32,272,128]{2,1,0:T(8,128)(2,1)S(1)}, u32[]{:S(2)}, u32[]{:S(2)}) async-start(bf16[32,272,128]{2,1,0:T(8,128)(2,1)} %pack.1), calls=%async_computation | async-start | bytes 4456448 | tf_op jit(solution)/shard_map/route_tiles/all_to_all | solution.py:236
  21.5 43.4 %all_gather.6 = bf16[8,80,128]{2,1,0:T(8,128)(2,1)S(1)} all-gather(bf16[1,80,128]{2,1,0:T(8,128)(2,1)S(1)} %constant_dynamic-slice_fusion), channel_id=1, replica_groups=mesh['zh'=8,'zl'=4,'y'=4,'x'=4,'core'=2] {'zh'}, dimensions={0}, use_global_device_ids=true | all-gather | bytes 184320 | tf_op jit(solution)/shard_map/gather_amplitudes/all_gather | solution.py:238
  64.8 16.6 %all_gather.7.refs_0_ = bf16[32,80,128]{2,1,0:T(8,128)(2,1)S(1)} all-gather(bf16[8,80,128]{2,1,0:T(8,128)(2,1)S(1)} %all_gather.6), channel_id=1, replica_groups=mesh['zh'=8,'zl'=4,'y'=4,'x'=4,'core'=2] {'zl'}, dimensions={0}, use_global_device_ids=true | all-gather | bytes 819200 | tf_op jit(solution)/shard_map/gather_amplitudes/all_gather | solution.py:238
  81.4 0.0 all-to-all-done.own_tiles
  81.4 1.9 %collective-permute-start = (bf16[32,272,128]{2,1,0:T(8,128)(2,1)S(1)}, bf16[32,272,128]{2,1,0:T(8,128)(2,1)S(1)}, u32[]{:S(2)}, u32[]{:S(2)}) collective-permute-start(bf16[32,272,128]{2,1,0:T(8,128)(2,1)S(1)} %all-to-all-done.own_tiles), channel_id=1, source_target_pairs={{0,1},{1,0},{2,3},{3,2},{4,5},{5,4},{6,7},{7,6},{8,9},{9,8},{10,11... | collective-permute-start | bytes 6684680 | tf_op jit(solution)/shard_map/share_tiles/ppermute | solution.py:242
  83.4 2.1 %collective-permute-start.1 = (bf16[32,80,128]{2,1,0:T(8,128)(2,1)S(1)}, bf16[32,80,128]{2,1,0:T(8,128)(2,1)S(1)}, u32[]{:S(2)}, u32[]{:S(2)}) collective-permute-start(bf16[32,80,128]{2,1,0:T(8,128)(2,1)S(1)} %all_gather.7.refs_0_), channel_id=1, source_target_pairs={{0,2},{1,9},{2,4},{3,11},{4,6},{5,13},{6,0},{7,15},{8,10},{9,17},{... | collective-permute-start | bytes 1966088 | tf_op jit(solution)/shard_map/gather_amplitudes/ppermute | solution.py:239
  85.5 4.3 %collective-permute-start.2 = (bf16[32,80,128]{2,1,0:T(8,128)(2,1)S(1)}, bf16[32,80,128]{2,1,0:T(8,128)(2,1)S(1)}, u32[]{:S(2)}, u32[]{:S(2)}) collective-permute-start(bf16[32,80,128]{2,1,0:T(8,128)(2,1)S(1)} %all_gather.7.refs_0_), channel_id=1, source_target_pairs={{0,4},{1,17},{2,6},{3,19},{4,0},{5,21},{6,2},{7,23},{8,12},{9,25},... | collective-permute-start | bytes 1966088 | tf_op jit(solution)/shard_map/gather_amplitudes/ppermute | solution.py:239
  89.7 2.1 %collective-permute-start.3 = (bf16[32,80,128]{2,1,0:T(8,128)(2,1)S(1)}, bf16[32,80,128]{2,1,0:T(8,128)(2,1)S(1)}, u32[]{:S(2)}, u32[]{:S(2)}) collective-permute-start(bf16[32,80,128]{2,1,0:T(8,128)(2,1)S(1)} %all_gather.7.refs_0_), channel_id=1, source_target_pairs={{0,6},{1,25},{2,0},{3,27},{4,2},{5,29},{6,4},{7,31},{8,14},{9,1},{... | collective-permute-start | bytes 1966088 | tf_op jit(solution)/shard_map/gather_amplitudes/ppermute | solution.py:239
  91.9 0.1 pad_add_fusion.place_ref
  92.0 0.0 collective-permute-done.far_tiles
  92.0 3.9 %cells.1.cells_ref = bf16[32,128,512]{2,1,0:T(8,128)(2,1)S(1)} custom-call(s32[32,2]{1,0:T(8,128)S(1)} %bitcast.4, s32[32,2]{1,0:T(8,128)S(1)} %bitcast.5, bf16[32,272,128]{2,1,0:T(8,128)(2,1)S(1)} %all-to-all-done.own_tiles, bf16[32,272,128]{2,1,0:T(8,128)(2,1)S(1)} %collective-permute-done.far_tiles), custom_call_target="tpu_custom_call" | custom-call | bytes 12582912 | tf_op jit(solution)/shard_map/product/cells/pallas_call | solution.py:111
  95.9 0.0 collective-permute-done.1.refs_1_
  95.9 3.6 %collective-permute-done.2.refs_2_ = bf16[32,80,128]{2,1,0:T(8,128)(2,1)S(1)} collective-permute-done((bf16[32,80,128]{2,1,0:T(8,128)(2,1)S(1)}, bf16[32,80,128]{2,1,0:T(8,128)(2,1)S(1)}, u32[]{:S(2)}, u32[]{:S(2)}) %collective-permute-start.2) | collective-permute-done | bytes 655392 | tf_op jit(solution)/shard_map/gather_amplitudes/ppermute | solution.py:239
  99.5 6.9 %collective-permute-done.3.refs_3_ = bf16[32,80,128]{2,1,0:T(8,128)(2,1)S(1)} collective-permute-done((bf16[32,80,128]{2,1,0:T(8,128)(2,1)S(1)}, bf16[32,80,128]{2,1,0:T(8,128)(2,1)S(1)}, u32[]{:S(2)}, u32[]{:S(2)}) %collective-permute-start.3) | collective-permute-done | bytes 655392 | tf_op jit(solution)/shard_map/gather_amplitudes/ppermute | solution.py:239
  106.5 2.3 %product.1 = f32[8,96,256]{2,1,0:T(8,128)S(1)} custom-call(s32[2]{0:T(128)S(1)} %pad_add_fusion.place_ref, bf16[32,128,512]{2,1,0:T(8,128)(2,1)S(1)} %cells.1.cells_ref, bf16[32,80,128]{2,1,0:T(8,128)(2,1)S(1)} %all_gather.7.refs_0_, bf16[32,80,128]{2,1,0:T(8,128)(2,1)S(1)} %collective-permute-done.1.refs_1_, ...), custom_call_target="tpu_custom_call" | custom-call | flops 1342177280 | bytes 8388608 | tf_op jit(solution)/shard_map/product/product/pallas_call | solution.py:156
  108.8 0.1 convert_element_type.26
  108.8 15.9 %all_to_all.15 = f16[8,96,256]{2,1,0:T(8,128)(2,1)S(1)} all-to-all(f16[8,96,256]{2,1,0:T(8,128)(2,1)S(1)} %convert_element_type.26), channel_id=1, replica_groups=mesh['zh'=8,'zl'=4,'y'=4,'x'=4,'core'=2] {'zl','core'}, dimensions={0} | all-to-all | bytes 786432 | tf_op jit(solution)/shard_map/reduce/all_to_all | solution.py:211
  124.7 1.0 convert_element_type.27.in_ref
  125.7 1.9 %near_sum.1 = f32[8,24,256]{2,1,0:T(8,128)} custom-call(f32[8,96,256]{2,1,0:T(8,128)} %convert_element_type.27.in_ref), custom_call_target="tpu_custom_call" | custom-call | flops 196608 | bytes 786432 | tf_op jit(solution)/shard_map/reduce/near_sum/pallas_call | solution.py:200
  127.6 0.9 convert_element_type.28
  128.5 38.1 %all_to_all.16 = f16[8,24,256]{2,1,0:T(8,128)(2,1)S(1)} all-to-all(f16[8,24,256]{2,1,0:T(8,128)(2,1)S(1)} %convert_element_type.28), channel_id=1, replica_groups=mesh['zh'=8,'zl'=4,'y'=4,'x'=4,'core'=2] {'zh'}, dimensions={0} | all-to-all | bytes 196608 | tf_op jit(solution)/shard_map/reduce/all_to_all | solution.py:211
  166.6 0.7 convert_element_type.29.in_ref
  167.3 1.6 far_sum.1
  (3 shorter events, 0.0 us)
Async XLA Ops:
  0.0 0.9 copy-start
  4.5 76.9 %all-to-all-start = ((bf16[32,272,128]{2,1,0:T(8,128)(2,1)}), bf16[32,272,128]{2,1,0:T(8,128)(2,1)S(1)}, u32[]{:S(2)}, u32[]{:S(2)}) async-start(bf16[32,272,128]{2,1,0:T(8,128)(2,1)} %pack.1), calls=%async_computation | async-start | bytes 4456448 | tf_op jit(solution)/shard_map/route_tiles/all_to_all | solution.py:236
  81.4 10.5 %collective-permute-start = (bf16[32,272,128]{2,1,0:T(8,128)(2,1)S(1)}, bf16[32,272,128]{2,1,0:T(8,128)(2,1)S(1)}, u32[]{:S(2)}, u32[]{:S(2)}) collective-permute-start(bf16[32,272,128]{2,1,0:T(8,128)(2,1)S(1)} %all-to-all-done.own_tiles), channel_id=1, source_target_pairs={{0,1},{1,0},{2,3},{3,2},{4,5},{5,4},{6,7},{7,6},{8,9},{9,8},{10,11... | collective-permute-start | bytes 6684680 | tf_op jit(solution)/shard_map/share_tiles/ppermute | solution.py:242
  83.4 12.5 %collective-permute-start.1 = (bf16[32,80,128]{2,1,0:T(8,128)(2,1)S(1)}, bf16[32,80,128]{2,1,0:T(8,128)(2,1)S(1)}, u32[]{:S(2)}, u32[]{:S(2)}) collective-permute-start(bf16[32,80,128]{2,1,0:T(8,128)(2,1)S(1)} %all_gather.7.refs_0_), channel_id=1, source_target_pairs={{0,2},{1,9},{2,4},{3,11},{4,6},{5,13},{6,0},{7,15},{8,10},{9,17},{... | collective-permute-start | bytes 1966088 | tf_op jit(solution)/shard_map/gather_amplitudes/ppermute | solution.py:239
  85.5 14.1 %collective-permute-start.2 = (bf16[32,80,128]{2,1,0:T(8,128)(2,1)S(1)}, bf16[32,80,128]{2,1,0:T(8,128)(2,1)S(1)}, u32[]{:S(2)}, u32[]{:S(2)}) collective-permute-start(bf16[32,80,128]{2,1,0:T(8,128)(2,1)S(1)} %all_gather.7.refs_0_), channel_id=1, source_target_pairs={{0,4},{1,17},{2,6},{3,19},{4,0},{5,21},{6,2},{7,23},{8,12},{9,25},... | collective-permute-start | bytes 1966088 | tf_op jit(solution)/shard_map/gather_amplitudes/ppermute | solution.py:239
  89.7 16.7 %collective-permute-start.3 = (bf16[32,80,128]{2,1,0:T(8,128)(2,1)S(1)}, bf16[32,80,128]{2,1,0:T(8,128)(2,1)S(1)}, u32[]{:S(2)}, u32[]{:S(2)}) collective-permute-start(bf16[32,80,128]{2,1,0:T(8,128)(2,1)S(1)} %all_gather.7.refs_0_), channel_id=1, source_target_pairs={{0,6},{1,25},{2,0},{3,27},{4,2},{5,29},{6,4},{7,31},{8,14},{9,1},{... | collective-permute-start | bytes 1966088 | tf_op jit(solution)/shard_map/gather_amplitudes/ppermute | solution.py:239

commit v3 on v2

--- a/solution.py
+++ b/solution.py
@@ -6,10 +6,12 @@
 from jax.sharding import Mesh, PartitionSpec as P
 
 CAP = 2
+AB = 2
 TILE = 128
 ZH, ZL, NY, NX, NC = 8, 4, 4, 4, 2
 Z, G = ("zh", "zl"), ("y", "x", "core")
 PIECES = 4
+ORDER = (3, 1, 2, 0)
 LABEL_ROWS = 16
 MESSAGE = CAP * TILE + LABEL_ROWS
 MIB = 1 << 20
@@ -99,8 +101,8 @@
         def _(g):
             for n in range(CAP):
                 label = labels[g, n]
-                for b in range(2):
-                    column = (c * CAP + b) * TILE
+                for b in range(AB):
+                    column = (c * AB + b) * TILE
 
                     @pl.when((label >= 0) & ((label & 1) == b))
                     def _():
@@ -110,7 +112,7 @@
 def cells(own_label, far_label, own_tiles, far_tiles, n_cd):
     return pl.pallas_call(
         cells_kernel,
-        out_shape=jax.ShapeDtypeStruct((n_cd, TILE, NC * CAP * TILE), own_tiles.dtype),
+        out_shape=jax.ShapeDtypeStruct((n_cd, TILE, NC * AB * TILE), own_tiles.dtype),
         in_specs=[SMEM, SMEM, VMEM, VMEM],
         out_specs=VMEM,
         compiler_params=pltpu.CompilerParams(vmem_limit_bytes=16 * MIB),
@@ -119,10 +121,24 @@
     )(own_label, far_label, own_tiles, far_tiles)
 
 
-def product_kernel(place_ref, cells_ref, *refs):
-    pieces, (out_ref, sorted_rows) = refs[:PIECES], refs[PIECES:]
+def encode(values):
+    peak = jnp.maximum(jnp.max(jnp.abs(values), axis=0, keepdims=True), TINY)
+    power = jnp.ceil(jnp.log2(jnp.broadcast_to(peak, (8, values.shape[1]))))
+    return jnp.floor(values * jnp.exp2(TOP - power)[:1] + 0.5), power[:1]
+
+
+def decode(codes, power):
+    return codes * jnp.exp2(jnp.broadcast_to(power - TOP, (8, codes.shape[1])))[:1]
+
+
+def widen(codes):
+    return codes.astype(jnp.int32).astype(jnp.float32)
+
+
+def product_kernel(place_ref, *refs):
+    pieces, (cells_ref, out_ref, sorted_rows, staged) = refs[:PIECES], refs[PIECES:]
     core, place = place_ref[0], place_ref[1]
-    width = CAP * TILE
+    width = AB * TILE
     size = pieces[0].shape[1]
     acc = None
     for i in range(0, cells_ref.shape[0], PER):
@@ -132,12 +148,9 @@
         rhs = cells_ref[i : i + PER].reshape(PER * TILE, NC * width)
         part = jnp.dot(lhs, rhs, preferred_element_type=jnp.float32)
         acc = part if acc is None else acc + part
-    peak = jnp.maximum(jnp.max(jnp.abs(acc)), TINY)
-    power = jnp.ceil(jnp.log2(jnp.full((MARGIN, width), peak, jnp.float32)))
-    scale = jnp.exp2(TOP - power)[:1, :1]
-    for d in range(PIECES):
-        row = pl.multiple_of(((place - d) & (PIECES - 1)) * size, size)
-        sorted_rows[pl.ds(row, size), :] = acc[d * size : (d + 1) * size] * scale
+    for i, d in enumerate(ORDER):
+        row = pl.multiple_of((place ^ d) * size, size)
+        sorted_rows[pl.ds(row, size), :] = acc[i * size : (i + 1) * size]
     block = acc.shape[0] // ZL
     rows = 2 * block // ZH
     for c in range(NC):
@@ -146,77 +159,95 @@
             for h in range(ZH // NC):
                 z = h * ZL + zl
                 value = sorted_rows[z * rows : (z + 1) * rows, c * width : (c + 1) * width]
-                out_ref[zl * NC + group, h * rows : (h + 1) * rows, :] = value
-            out_ref[zl * NC + group, block:, :] = power
+                staged[zl, h * rows : (h + 1) * rows, :] = value
+            codes, power = encode(staged[zl])
+            out_ref[zl * NC + group, :block, :] = codes.astype(jnp.int32).astype(out_ref.dtype)
+            power = jnp.broadcast_to(power, (MARGIN, width)).astype(jnp.int32)
+            out_ref[zl * NC + group, block:, :] = power.astype(out_ref.dtype)
 
 
 def product(place, filled, pieces):
     half = PIECES * pieces[0].shape[1]
-    out = (ZL * NC, half // ZL + MARGIN, CAP * TILE)
+    out = (ZL * NC, half // ZL + MARGIN, AB * TILE)
     return pl.pallas_call(
         product_kernel,
-        out_shape=jax.ShapeDtypeStruct(out, jnp.float32),
+        out_shape=jax.ShapeDtypeStruct(out, jnp.int16),
         in_specs=[SMEM] + [VMEM] * (1 + PIECES),
         out_specs=VMEM,
-        scratch_shapes=[pltpu.VMEM((half, NC * CAP * TILE), jnp.float32)],
+        scratch_shapes=[
+            pltpu.VMEM((half, NC * AB * TILE), jnp.float32),
+            pltpu.VMEM((ZL, half // ZL, AB * TILE), jnp.float32),
+        ],
         compiler_params=pltpu.CompilerParams(vmem_limit_bytes=16 * MIB),
         cost_estimate=pl.CostEstimate(
             flops=2 * half * filled.size, bytes_accessed=8 * MIB, transcendentals=0
         ),
         name="product",
-    )(place, filled, *pieces)
-
-
-def near_kernel(in_ref, out_ref):
+    )(place, *pieces, filled)
+
+
+def near_kernel(in_ref, out_ref, staged):
     block = in_ref.shape[1] - MARGIN
     rows = NC * block // ZH
-    power = in_ref[0, block : block + 8, :]
-    for s in range(1, ZL * NC):
-        power = jnp.maximum(power, in_ref[s, block : block + 8, :])
-    power = power + 2
     for c in range(NC):
         total = None
         for zl in range(ZL):
-            s = zl * NC + c
-            scale = jnp.exp2(in_ref[s, block : block + 8, :] - power)[:1]
-            term = in_ref[s, :block, :] * scale
+            codes = widen(in_ref[zl * NC + c])
+            term = decode(codes[:block], codes[block : block + 1])
             total = term if total is None else total + term
+        codes, power = encode(total)
         for h in range(ZH // NC):
             zh = c * (ZH // NC) + h
-            out_ref[zh, :rows, :] = total[h * rows : (h + 1) * rows]
-            out_ref[zh, rows:, :] = power[: out_ref.shape[1] - rows]
+            staged[zh, :rows, :] = codes[h * rows : (h + 1) * rows]
+            staged[zh, rows:, :] = jnp.broadcast_to(power, (staged.shape[1] - rows, power.shape[1]))
+    out_ref[...] = staged[...].astype(jnp.int32).astype(out_ref.dtype)
+
+
+def near_sum(value, rows):
+    out = (ZH, rows, value.shape[2])
+    return pl.pallas_call(
+        near_kernel,
+        out_shape=jax.ShapeDtypeStruct(out, value.dtype),
+        in_specs=[VMEM],
+        out_specs=VMEM,
+        scratch_shapes=[pltpu.VMEM(out, jnp.float32)],
+        cost_estimate=pl.CostEstimate(flops=value.size, bytes_accessed=3 * value.size, transcendentals=0),
+        name="near_sum",
+    )(value)
 
 
 def far_kernel(in_ref, out_ref):
     rows = out_ref.shape[0]
     total = None
     for zh in range(ZH):
-        term = in_ref[zh, :rows, :] * jnp.exp2(in_ref[zh, rows : rows + 1, :] - TOP)
+        codes = widen(in_ref[zh])
+        term = decode(codes[:rows], codes[rows : rows + 1])
         total = term if total is None else total + term
     out_ref[...] = total
 
 
-def local_sum(kernel, value, shape, name):
-    return pl.pallas_call(
-        kernel,
-        out_shape=jax.ShapeDtypeStruct(shape, jnp.float32),
+def far_sum(value, rows):
+    return pl.pallas_call(
+        far_kernel,
+        out_shape=jax.ShapeDtypeStruct((rows, value.shape[2]), jnp.float32),
         in_specs=[VMEM],
         out_specs=VMEM,
-        cost_estimate=pl.CostEstimate(flops=value.size, bytes_accessed=4 * value.size, transcendentals=0),
-        name=name,
+        cost_estimate=pl.CostEstimate(flops=value.size, bytes_accessed=3 * value.size, transcendentals=0),
+        name="far_sum",
     )(value)
 
 
-def narrow_all_to_all(value, axes):
-    sent = lax.all_to_all(value.astype(jnp.float16), axes, 0, 0, tiled=True)
-    return sent.astype(jnp.float32)
+def corner(at, core):
+    return (at + core) & 1
 
 
 def step(d):
     pairs = []
     for y in range(NY):
         for x in range(NX):
-            for core, (to_y, to_x) in enumerate(((y, (x + d) % NX), ((y + d) % NY, x))):
+            for core in range(NC):
+                to_x = (((x + core) ^ (d & 1)) - core) % NX
+                to_y = (((y + core) ^ (d >> 1)) - core) % NY
                 pairs.append(((y * NX + x) * NC + core, (to_y * NX + to_x) * NC + core))
     return pairs
 
@@ -226,17 +257,18 @@
     core, x, y = (lax.axis_index(a) for a in ("core", "x", "y"))
     rows = amplitudes.shape[1] // (ZH * ZL)
     half = amplitudes.shape[1] // NC
-    place = jnp.where(core == 0, x, y)
+    place = corner(x, core) + 2 * corner(y, core)
     with jax.named_scope("pack"):
         size = half // PIECES
+        outgoing = pack(task_cd, task_ab, owner_map, integrals, groups)
+        outgoing, amplitudes = lax.optimization_barrier((outgoing, amplitudes))
         share = lax.dynamic_slice_in_dim(amplitudes, core * half + place * size, size, 1)
-        outgoing = pack(task_cd, task_ab, owner_map, integrals, groups)
-        outgoing, share = lax.optimization_barrier((outgoing, share))
     with jax.named_scope("route_tiles"):
         own_tiles = lax.all_to_all(outgoing, G, 0, 0, tiled=True)
     with jax.named_scope("gather_amplitudes"):
         gathered = lax.all_gather(lax.all_gather(share, "zh", axis=0, tiled=True), "zl", axis=0, tiled=True)
-        pieces = [gathered] + [lax.ppermute(gathered, G, step(d)) for d in range(1, PIECES)]
+        both, along_x, along_y = (lax.ppermute(gathered, G, step(d)) for d in ORDER[:3])
+        pieces = [both, along_x, along_y, gathered]
     with jax.named_scope("share_tiles"):
         own_tiles, _ = lax.optimization_barrier((own_tiles, gathered))
         far_tiles = lax.ppermute(own_tiles, "core", [(0, 1), (1, 0)])
@@ -245,10 +277,9 @@
         filled = cells(own_label, far_label, own_tiles, far_tiles, ZH * ZL)
         partial = product(jnp.stack([core, place]), filled, pieces)
     with jax.named_scope("reduce"):
-        near = narrow_all_to_all(partial, ("zl", "core"))
-        near = local_sum(near_kernel, near, (ZH, rows + 4, CAP * TILE), "near_sum")
-        far = narrow_all_to_all(near, "zh")
-        return local_sum(far_kernel, far, (rows, CAP * TILE), "far_sum")
+        near = lax.all_to_all(partial, ("zl", "core"), 0, 0, tiled=True)
+        near = near_sum(near, rows + 4)
+        return far_sum(lax.all_to_all(near, "zh", 0, 0, tiled=True), rows)
 
 
 def solution(mesh):

time: 170 us -> 165 us (0.971)
  waiting for transfers between devices: 10.6 us -> 7.16 us
  other arithmetic: 2.76 us -> 0.11 us
  blocking collectives: 114 us -> 116 us
    ppermute x3, waiting for transfers between devices: 10.6 us -> 7.16 us  [on_device(): lax.ppermute(gathered, G, step(d))]
    convert_element_type x4 -> x0, other arithmetic: 2.65 us -> none  [the longest x2 1.64 us: narrow_all_to_all(): return sent.astype(jnp.float32)]
    all_to_all x2, blocking collectives: 54 us -> 55.8 us  [the longest x1 38.4 us: on_device(): return far_sum(lax.all_to_all(near, 'zh', 0, 0, tiled=True), rows)]
  transfers between devices with their start and end apart: 5 -> 5, of which waited for: 2 -> 3; matrix products, arithmetic and copies ran while one was open for 0% -> 0% of each run, Pallas kernels for 2% -> 2%
where the time goes in v3:
time: 165 us; the launch traced here: 164 us
  blocking collectives  116 us (70%)
  starting transfers between devices  28 us (17%)
  Pallas kernels  13.2 us (8%)
  waiting for transfers between devices  7.16 us (4%)
    all_gather x1, blocking collectives, on_device(): lax.all_gather(share, 'zh', axis=0, tiled=True)  43.3 us
    all_to_all x1, blocking collectives, on_device(): return far_sum(lax.all_to_all(near, 'zh', 0, 0, tiled=True), rows)  38.4 us
    all_to_all x1, blocking collectives, on_device(): near = lax.all_to_all(partial, ('zl', 'core'), 0, 0, tiled=True)  17.4 us
    all_to_all x1, starting transfers between devices, on_device(): own_tiles = lax.all_to_all(outgoing, G, 0, 0, tiled=True)  16.9 us
    all_gather x1, blocking collectives, on_device(): lax.all_gather(lax.all_gather(share, 'zh', axis=0, tiled=True), 'zl', axi...  16.6 us
    ppermute x3, starting transfers between devices, on_device(): lax.ppermute(gathered, G, step(d))  9.21 us
    ppermute x3, waiting for transfers between devices, on_device(): lax.ppermute(gathered, G, step(d))  7.16 us
    pallas_call x1, Pallas kernels, cells(): pl.pallas_call(cells_kernel, out_shape=jax.ShapeDtypeStruct((n_cd, TILE,...  3.87 us
  transfers between devices with their start and end apart: 5, of which 3 were waited for; matrix products, arithmetic and copies ran while one was open for 0% of the time, Pallas kernels for 2%

profile of v3, /device:TPU:6, one launch (start us, length us, event | category | flops | bytes accessed | tf_op | source)
XLA Modules:
  0.0 164.3 jit_solution(15977508223213298382)
XLA Ops:
  0.0 0.0 copy-start
  0.0 3.7 %pack.1 = bf16[32,272,128]{2,1,0:T(8,128)(2,1)} custom-call(s32[32]{0:T(128)} %cd_ref.1, s32[32]{0:T(128)} %ab_ref.1, s32[64]{0:T(128)} %owner_ref.1, bf16[32,128,128]{2,1,0:T(8,128)(2,1)} %tiles_ref.1), custom_call_target="tpu_custom_call" | custom-call | bytes 3145728 | tf_op jit(solution)/shard_map/pack/pack/pallas_call | solution.py:76
  3.7 16.9 %all-to-all-start = ((bf16[32,272,128]{2,1,0:T(8,128)(2,1)}), bf16[32,272,128]{2,1,0:T(8,128)(2,1)S(1)}, u32[]{:S(2)}, u32[]{:S(2)}) async-start(bf16[32,272,128]{2,1,0:T(8,128)(2,1)} %pack.1), calls=%async_computation | async-start | bytes 4456448 | tf_op jit(solution)/shard_map/route_tiles/all_to_all | solution.py:267
  20.7 0.0 copy-done
  20.7 43.3 %all_gather.6 = bf16[8,80,128]{2,1,0:T(8,128)(2,1)S(1)} all-gather(bf16[1,80,128]{2,1,0:T(8,128)(2,1)S(1)} %constant_dynamic-slice_fusion), channel_id=1, replica_groups=mesh['zh'=8,'zl'=4,'y'=4,'x'=4,'core'=2] {'zh'}, dimensions={0}, use_global_device_ids=true | all-gather | bytes 184320 | tf_op jit(solution)/shard_map/gather_amplitudes/all_gather | solution.py:269
  64.0 16.6 %all_gather.7.refs_3_ = bf16[32,80,128]{2,1,0:T(8,128)(2,1)S(1)} all-gather(bf16[8,80,128]{2,1,0:T(8,128)(2,1)S(1)} %all_gather.6), channel_id=1, replica_groups=mesh['zh'=8,'zl'=4,'y'=4,'x'=4,'core'=2] {'zl'}, dimensions={0}, use_global_device_ids=true | all-gather | bytes 819200 | tf_op jit(solution)/shard_map/gather_amplitudes/all_gather | solution.py:269
  80.6 0.0 all-to-all-done.own_tiles
  80.6 1.9 %collective-permute-start.3 = (bf16[32,272,128]{2,1,0:T(8,128)(2,1)S(1)}, bf16[32,272,128]{2,1,0:T(8,128)(2,1)S(1)}, u32[]{:S(2)}, u32[]{:S(2)}) collective-permute-start(bf16[32,272,128]{2,1,0:T(8,128)(2,1)S(1)} %all-to-all-done.own_tiles), channel_id=1, source_target_pairs={{0,1},{1,0},{2,3},{3,2},{4,5},{5,4},{6,7},{7,6},{8,9},{9,8},{10,11... | collective-permute-start | bytes 6684680 | tf_op jit(solution)/shard_map/share_tiles/ppermute | solution.py:274
  82.5 3.2 %collective-permute-start = (bf16[32,80,128]{2,1,0:T(8,128)(2,1)S(1)}, bf16[32,80,128]{2,1,0:T(8,128)(2,1)S(1)}, u32[]{:S(2)}, u32[]{:S(2)}) collective-permute-start(bf16[32,80,128]{2,1,0:T(8,128)(2,1)S(1)} %all_gather.7.refs_3_), channel_id=1, source_target_pairs={{0,10},{1,31},{2,8},{3,29},{4,14},{5,27},{6,12},{7,25},{8,2},{9,23... | collective-permute-start | bytes 1966088 | tf_op jit(solution)/shard_map/gather_amplitudes/ppermute | solution.py:270
  85.7 3.3 %collective-permute-start.1 = (bf16[32,80,128]{2,1,0:T(8,128)(2,1)S(1)}, bf16[32,80,128]{2,1,0:T(8,128)(2,1)S(1)}, u32[]{:S(2)}, u32[]{:S(2)}) collective-permute-start(bf16[32,80,128]{2,1,0:T(8,128)(2,1)S(1)} %all_gather.7.refs_3_), channel_id=1, source_target_pairs={{0,2},{1,7},{2,0},{3,5},{4,6},{5,3},{6,4},{7,1},{8,10},{9,15},{10,... | collective-permute-start | bytes 1966088 | tf_op jit(solution)/shard_map/gather_amplitudes/ppermute | solution.py:270
  89.1 2.7 %collective-permute-start.2 = (bf16[32,80,128]{2,1,0:T(8,128)(2,1)S(1)}, bf16[32,80,128]{2,1,0:T(8,128)(2,1)S(1)}, u32[]{:S(2)}, u32[]{:S(2)}) collective-permute-start(bf16[32,80,128]{2,1,0:T(8,128)(2,1)S(1)} %all_gather.7.refs_3_), channel_id=1, source_target_pairs={{0,8},{1,25},{2,10},{3,27},{4,12},{5,29},{6,14},{7,31},{8,0},{9,17... | collective-permute-start | bytes 1966088 | tf_op jit(solution)/shard_map/gather_amplitudes/ppermute | solution.py:270
  91.8 0.1 pad_add_fusion.place_ref
  91.9 0.0 collective-permute-done.3.far_tiles
  91.9 3.9 %cells.1.refs_4_ = bf16[32,128,512]{2,1,0:T(8,128)(2,1)S(1)} custom-call(s32[32,2]{1,0:T(8,128)S(1)} %bitcast.4, s32[32,2]{1,0:T(8,128)S(1)} %bitcast.5, bf16[32,272,128]{2,1,0:T(8,128)(2,1)S(1)} %all-to-all-done.own_tiles, bf16[32,272,128]{2,1,0:T(8,128)(2,1)S(1)} %collective-permute-done.3.far_tiles), custom_call_target="tpu_custom_call" | custom-call | bytes 12582912 | tf_op jit(solution)/shard_map/product/cells/pallas_call | solution.py:113
  95.8 0.2 collective-permute-done.refs_0_
  96.0 6.7 %collective-permute-done.1.refs_1_ = bf16[32,80,128]{2,1,0:T(8,128)(2,1)S(1)} collective-permute-done((bf16[32,80,128]{2,1,0:T(8,128)(2,1)S(1)}, bf16[32,80,128]{2,1,0:T(8,128)(2,1)S(1)}, u32[]{:S(2)}, u32[]{:S(2)}) %collective-permute-start.1) | collective-permute-done | bytes 655392 | tf_op jit(solution)/shard_map/gather_amplitudes/ppermute | solution.py:270
  102.7 0.2 collective-permute-done.2.refs_2_
  102.9 2.3 %product.1 = s16[8,96,256]{2,1,0:T(8,128)(2,1)S(1)} custom-call(s32[2]{0:T(128)S(1)} %pad_add_fusion.place_ref, bf16[32,80,128]{2,1,0:T(8,128)(2,1)S(1)} %collective-permute-done.refs_0_, bf16[32,80,128]{2,1,0:T(8,128)(2,1)S(1)} %collective-permute-done.1.refs_1_, bf16[32,80,128]{2,1,0:T(8,128)(2,1)S(1)} %collective-permute-done.2.refs_2_, ...), custom_call_target="tpu_custom_call" | custom-call | flops 1342177280 | bytes 8388608 | tf_op jit(solution)/shard_map/product/product/pallas_call | solution.py:172
  105.2 17.4 %all_to_all.15.in_ref = s16[8,96,256]{2,1,0:T(8,128)(2,1)} all-to-all(s16[8,96,256]{2,1,0:T(8,128)(2,1)S(1)} %product.1), channel_id=1, replica_groups=mesh['zh'=8,'zl'=4,'y'=4,'x'=4,'core'=2] {'zl','core'}, dimensions={0} | all-to-all | bytes 786432 | tf_op jit(solution)/shard_map/reduce/all_to_all | solution.py:280
  122.6 1.8 %near_sum.1 = s16[8,24,256]{2,1,0:T(8,128)(2,1)} custom-call(s16[8,96,256]{2,1,0:T(8,128)(2,1)} %all_to_all.15.in_ref), custom_call_target="tpu_custom_call" | custom-call | flops 196608 | bytes 589824 | tf_op jit(solution)/shard_map/reduce/near_sum/pallas_call | solution.py:208
  124.4 38.4 %all_to_all.16.in_ref = s16[8,24,256]{2,1,0:T(8,128)(2,1)} all-to-all(s16[8,24,256]{2,1,0:T(8,128)(2,1)} %near_sum.1), channel_id=1, replica_groups=mesh['zh'=8,'zl'=4,'y'=4,'x'=4,'core'=2] {'zh'}, dimensions={0} | all-to-all | bytes 196608 | tf_op jit(solution)/shard_map/reduce/all_to_all | solution.py:282
  162.8 1.5 far_sum.1
  (3 shorter events, 0.0 us)
Async XLA Ops:
  0.0 20.7 %copy-start = (bf16[1,640,128]{2,1,0:T(8,128)(2,1)S(1)}, bf16[1,640,128]{2,1,0:T(8,128)(2,1)}, u32[]{:S(2)}) copy-start(bf16[1,640,128]{2,1,0:T(8,128)(2,1)} %param.5) | copy-start | bytes 491524
  3.7 76.9 %all-to-all-start = ((bf16[32,272,128]{2,1,0:T(8,128)(2,1)}), bf16[32,272,128]{2,1,0:T(8,128)(2,1)S(1)}, u32[]{:S(2)}, u32[]{:S(2)}) async-start(bf16[32,272,128]{2,1,0:T(8,128)(2,1)} %pack.1), calls=%async_computation | async-start | bytes 4456448 | tf_op jit(solution)/shard_map/route_tiles/all_to_all | solution.py:267
  80.6 11.3 %collective-permute-start.3 = (bf16[32,272,128]{2,1,0:T(8,128)(2,1)S(1)}, bf16[32,272,128]{2,1,0:T(8,128)(2,1)S(1)}, u32[]{:S(2)}, u32[]{:S(2)}) collective-permute-start(bf16[32,272,128]{2,1,0:T(8,128)(2,1)S(1)} %all-to-all-done.own_tiles), channel_id=1, source_target_pairs={{0,1},{1,0},{2,3},{3,2},{4,5},{5,4},{6,7},{7,6},{8,9},{9,8},{10,11... | collective-permute-start | bytes 6684680 | tf_op jit(solution)/shard_map/share_tiles/ppermute | solution.py:274
  82.5 13.5 %collective-permute-start = (bf16[32,80,128]{2,1,0:T(8,128)(2,1)S(1)}, bf16[32,80,128]{2,1,0:T(8,128)(2,1)S(1)}, u32[]{:S(2)}, u32[]{:S(2)}) collective-permute-start(bf16[32,80,128]{2,1,0:T(8,128)(2,1)S(1)} %all_gather.7.refs_3_), channel_id=1, source_target_pairs={{0,10},{1,31},{2,8},{3,29},{4,14},{5,27},{6,12},{7,25},{8,2},{9,23... | collective-permute-start | bytes 1966088 | tf_op jit(solution)/shard_map/gather_amplitudes/ppermute | solution.py:270
  85.7 17.0 %collective-permute-start.1 = (bf16[32,80,128]{2,1,0:T(8,128)(2,1)S(1)}, bf16[32,80,128]{2,1,0:T(8,128)(2,1)S(1)}, u32[]{:S(2)}, u32[]{:S(2)}) collective-permute-start(bf16[32,80,128]{2,1,0:T(8,128)(2,1)S(1)} %all_gather.7.refs_3_), channel_id=1, source_target_pairs={{0,2},{1,7},{2,0},{3,5},{4,6},{5,3},{6,4},{7,1},{8,10},{9,15},{10,... | collective-permute-start | bytes 1966088 | tf_op jit(solution)/shard_map/gather_amplitudes/ppermute | solution.py:270
  89.1 13.9 %collective-permute-start.2 = (bf16[32,80,128]{2,1,0:T(8,128)(2,1)S(1)}, bf16[32,80,128]{2,1,0:T(8,128)(2,1)S(1)}, u32[]{:S(2)}, u32[]{:S(2)}) collective-permute-start(bf16[32,80,128]{2,1,0:T(8,128)(2,1)S(1)} %all_gather.7.refs_3_), channel_id=1, source_target_pairs={{0,8},{1,25},{2,10},{3,27},{4,12},{5,29},{6,14},{7,31},{8,0},{9,17... | collective-permute-start | bytes 1966088 | tf_op jit(solution)/shard_map/gather_amplitudes/ppermute | solution.py:270

commit v4 on v3

--- a/solution.py
+++ b/solution.py
@@ -125,14 +125,6 @@
     peak = jnp.maximum(jnp.max(jnp.abs(values), axis=0, keepdims=True), TINY)
     power = jnp.ceil(jnp.log2(jnp.broadcast_to(peak, (8, values.shape[1]))))
     return jnp.floor(values * jnp.exp2(TOP - power)[:1] + 0.5), power[:1]
-
-
-def decode(codes, power):
-    return codes * jnp.exp2(jnp.broadcast_to(power - TOP, (8, codes.shape[1])))[:1]
-
-
-def widen(codes):
-    return codes.astype(jnp.int32).astype(jnp.float32)
 
 
 def product_kernel(place_ref, *refs):
@@ -186,55 +178,22 @@
     )(place, *pieces, filled)
 
 
-def near_kernel(in_ref, out_ref, staged):
-    block = in_ref.shape[1] - MARGIN
-    rows = NC * block // ZH
-    for c in range(NC):
-        total = None
-        for zl in range(ZL):
-            codes = widen(in_ref[zl * NC + c])
-            term = decode(codes[:block], codes[block : block + 1])
-            total = term if total is None else total + term
-        codes, power = encode(total)
-        for h in range(ZH // NC):
-            zh = c * (ZH // NC) + h
-            staged[zh, :rows, :] = codes[h * rows : (h + 1) * rows]
-            staged[zh, rows:, :] = jnp.broadcast_to(power, (staged.shape[1] - rows, power.shape[1]))
-    out_ref[...] = staged[...].astype(jnp.int32).astype(out_ref.dtype)
-
-
-def near_sum(value, rows):
-    out = (ZH, rows, value.shape[2])
-    return pl.pallas_call(
-        near_kernel,
-        out_shape=jax.ShapeDtypeStruct(out, value.dtype),
-        in_specs=[VMEM],
-        out_specs=VMEM,
-        scratch_shapes=[pltpu.VMEM(out, jnp.float32)],
-        cost_estimate=pl.CostEstimate(flops=value.size, bytes_accessed=3 * value.size, transcendentals=0),
-        name="near_sum",
-    )(value)
-
-
-def far_kernel(in_ref, out_ref):
-    rows = out_ref.shape[0]
-    total = None
-    for zh in range(ZH):
-        codes = widen(in_ref[zh])
-        term = decode(codes[:rows], codes[rows : rows + 1])
-        total = term if total is None else total + term
-    out_ref[...] = total
-
-
-def far_sum(value, rows):
-    return pl.pallas_call(
-        far_kernel,
-        out_shape=jax.ShapeDtypeStruct((rows, value.shape[2]), jnp.float32),
-        in_specs=[VMEM],
-        out_specs=VMEM,
-        cost_estimate=pl.CostEstimate(flops=value.size, bytes_accessed=3 * value.size, transcendentals=0),
-        name="far_sum",
-    )(value)
+def near_sum(codes, rows):
+    block = codes.shape[1] - MARGIN
+    width = codes.shape[2]
+    codes = codes.astype(jnp.float32).reshape(ZL, NC, block + MARGIN, width)
+    total = jnp.sum(codes[:, :, :block] * jnp.exp2(codes[:, :, block : block + 1] - TOP), axis=0)
+    peak = jnp.maximum(jnp.max(jnp.abs(total), axis=1, keepdims=True), TINY)
+    power = jnp.ceil(jnp.log2(peak))
+    codes = jnp.floor(total * jnp.exp2(TOP - power) + 0.5).reshape(ZH, NC * block // ZH, width)
+    power = jnp.repeat(power, ZH // NC, axis=0).reshape(ZH, 1, width)
+    power = jnp.broadcast_to(power, (ZH, rows - codes.shape[1], width))
+    return jnp.concatenate([codes, power], axis=1).astype(jnp.int32).astype(jnp.int16)
+
+
+def far_sum(codes, rows):
+    codes = codes.astype(jnp.float32)
+    return jnp.sum(codes[:, :rows] * jnp.exp2(codes[:, rows : rows + 1] - TOP), axis=0)
 
 
 def corner(at, core):

time: 165 us -> 162 us (0.982)
  Pallas kernels: 13.2 us -> 9.95 us
    pallas_call x2 -> x0, Pallas kernels: 3.33 us -> none  [the longest x1 1.79 us: near_sum(): pl.pallas_call(near_kernel, out_shape=jax.ShapeDtypeStruct(out, value.dty...]
where the time goes in v4:
time: 162 us
  blocking collectives  115 us (71%)
  starting transfers between devices  28 us (17%)
  Pallas kernels  9.95 us (6%)
  waiting for transfers between devices  7.12 us (4%)
    all_gather x1, blocking collectives, on_device(): lax.all_gather(share, 'zh', axis=0, tiled=True)  43.3 us
    all_to_all x1, blocking collectives, on_device(): return far_sum(lax.all_to_all(near, 'zh', 0, 0, tiled=True), rows)  37.9 us
    all_to_all x1, blocking collectives, on_device(): near = lax.all_to_all(partial, ('zl', 'core'), 0, 0, tiled=True)  17.3 us
    all_to_all x1, starting transfers between devices, on_device(): own_tiles = lax.all_to_all(outgoing, G, 0, 0, tiled=True)  16.9 us
    all_gather x1, blocking collectives, on_device(): lax.all_gather(lax.all_gather(share, 'zh', axis=0, tiled=True), 'zl', axi...  16.6 us
    ppermute x3, starting transfers between devices, on_device(): lax.ppermute(gathered, G, step(d))  9.21 us
    ppermute x3, waiting for transfers between devices, on_device(): lax.ppermute(gathered, G, step(d))  7.12 us
    pallas_call x1, Pallas kernels, cells(): pl.pallas_call(cells_kernel, out_shape=jax.ShapeDtypeStruct((n_cd, TILE,...  3.9 us
  transfers between devices with their start and end apart: 5, of which 3 were waited for; matrix products, arithmetic and copies ran while one was open for 0% of the time, Pallas kernels for 2%

profile of v4, /device:TPU:6, one launch (start us, length us, event | category | flops | bytes accessed | tf_op | source)
XLA Modules:
  0.0 161.7 jit_solution(17350573254737791814)
XLA Ops:
  0.0 0.0 copy-start
  0.0 3.8 %pack.1 = bf16[32,272,128]{2,1,0:T(8,128)(2,1)} custom-call(s32[32]{0:T(128)} %cd_ref.1, s32[32]{0:T(128)} %ab_ref.1, s32[64]{0:T(128)} %owner_ref.1, bf16[32,128,128]{2,1,0:T(8,128)(2,1)} %tiles_ref.1), custom_call_target="tpu_custom_call" | custom-call | bytes 3145728 | tf_op jit(solution)/shard_map/pack/pack/pallas_call | solution.py:76
  3.8 16.9 %all-to-all-start = ((bf16[32,272,128]{2,1,0:T(8,128)(2,1)}), bf16[32,272,128]{2,1,0:T(8,128)(2,1)S(1)}, u32[]{:S(2)}, u32[]{:S(2)}) async-start(bf16[32,272,128]{2,1,0:T(8,128)(2,1)} %pack.1), calls=%async_computation | async-start | bytes 4456448 | tf_op jit(solution)/shard_map/route_tiles/all_to_all | solution.py:226
  20.7 0.0 copy-done
  20.7 43.3 %all_gather.6 = bf16[8,80,128]{2,1,0:T(8,128)(2,1)S(1)} all-gather(bf16[1,80,128]{2,1,0:T(8,128)(2,1)S(1)} %constant_dynamic-slice_fusion), channel_id=1, replica_groups=mesh['zh'=8,'zl'=4,'y'=4,'x'=4,'core'=2] {'zh'}, dimensions={0}, use_global_device_ids=true | all-gather | bytes 184320 | tf_op jit(solution)/shard_map/gather_amplitudes/all_gather | solution.py:228
  64.0 16.6 %all_gather.7.refs_3_ = bf16[32,80,128]{2,1,0:T(8,128)(2,1)S(1)} all-gather(bf16[8,80,128]{2,1,0:T(8,128)(2,1)S(1)} %all_gather.6), channel_id=1, replica_groups=mesh['zh'=8,'zl'=4,'y'=4,'x'=4,'core'=2] {'zl'}, dimensions={0}, use_global_device_ids=true | all-gather | bytes 819200 | tf_op jit(solution)/shard_map/gather_amplitudes/all_gather | solution.py:228
  80.7 0.0 all-to-all-done.own_tiles
  80.7 1.9 %collective-permute-start.3 = (bf16[32,272,128]{2,1,0:T(8,128)(2,1)S(1)}, bf16[32,272,128]{2,1,0:T(8,128)(2,1)S(1)}, u32[]{:S(2)}, u32[]{:S(2)}) collective-permute-start(bf16[32,272,128]{2,1,0:T(8,128)(2,1)S(1)} %all-to-all-done.own_tiles), channel_id=1, source_target_pairs={{0,1},{1,0},{2,3},{3,2},{4,5},{5,4},{6,7},{7,6},{8,9},{9,8},{10,11... | collective-permute-start | bytes 6684680 | tf_op jit(solution)/shard_map/share_tiles/ppermute | solution.py:233
  82.6 3.3 %collective-permute-start = (bf16[32,80,128]{2,1,0:T(8,128)(2,1)S(1)}, bf16[32,80,128]{2,1,0:T(8,128)(2,1)S(1)}, u32[]{:S(2)}, u32[]{:S(2)}) collective-permute-start(bf16[32,80,128]{2,1,0:T(8,128)(2,1)S(1)} %all_gather.7.refs_3_), channel_id=1, source_target_pairs={{0,10},{1,31},{2,8},{3,29},{4,14},{5,27},{6,12},{7,25},{8,2},{9,23... | collective-permute-start | bytes 1966088 | tf_op jit(solution)/shard_map/gather_amplitudes/ppermute | solution.py:229
  85.9 3.0 %collective-permute-start.1 = (bf16[32,80,128]{2,1,0:T(8,128)(2,1)S(1)}, bf16[32,80,128]{2,1,0:T(8,128)(2,1)S(1)}, u32[]{:S(2)}, u32[]{:S(2)}) collective-permute-start(bf16[32,80,128]{2,1,0:T(8,128)(2,1)S(1)} %all_gather.7.refs_3_), channel_id=1, source_target_pairs={{0,2},{1,7},{2,0},{3,5},{4,6},{5,3},{6,4},{7,1},{8,10},{9,15},{10,... | collective-permute-start | bytes 1966088 | tf_op jit(solution)/shard_map/gather_amplitudes/ppermute | solution.py:229
  88.8 3.0 %collective-permute-start.2 = (bf16[32,80,128]{2,1,0:T(8,128)(2,1)S(1)}, bf16[32,80,128]{2,1,0:T(8,128)(2,1)S(1)}, u32[]{:S(2)}, u32[]{:S(2)}) collective-permute-start(bf16[32,80,128]{2,1,0:T(8,128)(2,1)S(1)} %all_gather.7.refs_3_), channel_id=1, source_target_pairs={{0,8},{1,25},{2,10},{3,27},{4,12},{5,29},{6,14},{7,31},{8,0},{9,17... | collective-permute-start | bytes 1966088 | tf_op jit(solution)/shard_map/gather_amplitudes/ppermute | solution.py:229
  91.8 0.1 pad_add_fusion.place_ref
  91.9 0.0 collective-permute-done.3.far_tiles
  92.0 3.9 %cells.1.refs_4_ = bf16[32,128,512]{2,1,0:T(8,128)(2,1)S(1)} custom-call(s32[32,2]{1,0:T(8,128)S(1)} %bitcast.13, s32[32,2]{1,0:T(8,128)S(1)} %bitcast.14, bf16[32,272,128]{2,1,0:T(8,128)(2,1)S(1)} %all-to-all-done.own_tiles, bf16[32,272,128]{2,1,0:T(8,128)(2,1)S(1)} %collective-permute-done.3.far_tiles), custom_call_target="tpu_custom_call" | custom-call | bytes 12582912 | tf_op jit(solution)/shard_map/product/cells/pallas_call | solution.py:113
  95.9 0.2 collective-permute-done.refs_0_
  96.1 6.4 %collective-permute-done.1.refs_1_ = bf16[32,80,128]{2,1,0:T(8,128)(2,1)S(1)} collective-permute-done((bf16[32,80,128]{2,1,0:T(8,128)(2,1)S(1)}, bf16[32,80,128]{2,1,0:T(8,128)(2,1)S(1)}, u32[]{:S(2)}, u32[]{:S(2)}) %collective-permute-start.1) | collective-permute-done | bytes 655392 | tf_op jit(solution)/shard_map/gather_amplitudes/ppermute | solution.py:229
  102.5 0.5 collective-permute-done.2.refs_2_
  103.0 2.3 %product.1 = s16[8,96,256]{2,1,0:T(8,128)(2,1)S(1)} custom-call(s32[2]{0:T(128)S(1)} %pad_add_fusion.place_ref, bf16[32,80,128]{2,1,0:T(8,128)(2,1)S(1)} %collective-permute-done.refs_0_, bf16[32,80,128]{2,1,0:T(8,128)(2,1)S(1)} %collective-permute-done.1.refs_1_, bf16[32,80,128]{2,1,0:T(8,128)(2,1)S(1)} %collective-permute-done.2.refs_2_, ...), custom_call_target="tpu_custom_call" | custom-call | flops 1342177280 | bytes 8388608 | tf_op jit(solution)/shard_map/product/product/pallas_call | solution.py:164
  105.3 17.3 %all_to_all.15 = s16[8,96,256]{2,1,0:T(8,128)(2,1)S(1)} all-to-all(s16[8,96,256]{2,1,0:T(8,128)(2,1)S(1)} %product.1), channel_id=1, replica_groups=mesh['zh'=8,'zl'=4,'y'=4,'x'=4,'core'=2] {'zl','core'}, dimensions={0} | all-to-all | bytes 786432 | tf_op jit(solution)/shard_map/reduce/all_to_all | solution.py:239
  122.6 0.1 bitcast_convert_fusion
  122.7 0.1 fusion
  123.0 37.9 %all_to_all.16 = s16[8,24,256]{2,1,0:T(8,128)(2,1)S(1)} all-to-all(s16[8,24,256]{2,1,0:T(8,128)(2,1)S(1)} %fusion.2), channel_id=1, replica_groups=mesh['zh'=8,'zl'=4,'y'=4,'x'=4,'core'=2] {'zh'}, dimensions={0} | all-to-all | bytes 196608 | tf_op jit(solution)/shard_map/reduce/all_to_all | solution.py:241
  161.0 0.6 fusion.1
  (18 shorter events, 0.3 us)
Async XLA Ops:
  0.0 20.7 %copy-start = (bf16[1,640,128]{2,1,0:T(8,128)(2,1)S(1)}, bf16[1,640,128]{2,1,0:T(8,128)(2,1)}, u32[]{:S(2)}) copy-start(bf16[1,640,128]{2,1,0:T(8,128)(2,1)} %param.5) | copy-start | bytes 491524
  3.8 76.9 %all-to-all-start = ((bf16[32,272,128]{2,1,0:T(8,128)(2,1)}), bf16[32,272,128]{2,1,0:T(8,128)(2,1)S(1)}, u32[]{:S(2)}, u32[]{:S(2)}) async-start(bf16[32,272,128]{2,1,0:T(8,128)(2,1)} %pack.1), calls=%async_computation | async-start | bytes 4456448 | tf_op jit(solution)/shard_map/route_tiles/all_to_all | solution.py:226
  80.7 11.3 %collective-permute-start.3 = (bf16[32,272,128]{2,1,0:T(8,128)(2,1)S(1)}, bf16[32,272,128]{2,1,0:T(8,128)(2,1)S(1)}, u32[]{:S(2)}, u32[]{:S(2)}) collective-permute-start(bf16[32,272,128]{2,1,0:T(8,128)(2,1)S(1)} %all-to-all-done.own_tiles), channel_id=1, source_target_pairs={{0,1},{1,0},{2,3},{3,2},{4,5},{5,4},{6,7},{7,6},{8,9},{9,8},{10,11... | collective-permute-start | bytes 6684680 | tf_op jit(solution)/shard_map/share_tiles/ppermute | solution.py:233
  82.6 13.5 %collective-permute-start = (bf16[32,80,128]{2,1,0:T(8,128)(2,1)S(1)}, bf16[32,80,128]{2,1,0:T(8,128)(2,1)S(1)}, u32[]{:S(2)}, u32[]{:S(2)}) collective-permute-start(bf16[32,80,128]{2,1,0:T(8,128)(2,1)S(1)} %all_gather.7.refs_3_), channel_id=1, source_target_pairs={{0,10},{1,31},{2,8},{3,29},{4,14},{5,27},{6,12},{7,25},{8,2},{9,23... | collective-permute-start | bytes 1966088 | tf_op jit(solution)/shard_map/gather_amplitudes/ppermute | solution.py:229
  85.9 16.6 %collective-permute-start.1 = (bf16[32,80,128]{2,1,0:T(8,128)(2,1)S(1)}, bf16[32,80,128]{2,1,0:T(8,128)(2,1)S(1)}, u32[]{:S(2)}, u32[]{:S(2)}) collective-permute-start(bf16[32,80,128]{2,1,0:T(8,128)(2,1)S(1)} %all_gather.7.refs_3_), channel_id=1, source_target_pairs={{0,2},{1,7},{2,0},{3,5},{4,6},{5,3},{6,4},{7,1},{8,10},{9,15},{10,... | collective-permute-start | bytes 1966088 | tf_op jit(solution)/shard_map/gather_amplitudes/ppermute | solution.py:229
  88.8 14.2 %collective-permute-start.2 = (bf16[32,80,128]{2,1,0:T(8,128)(2,1)S(1)}, bf16[32,80,128]{2,1,0:T(8,128)(2,1)S(1)}, u32[]{:S(2)}, u32[]{:S(2)}) collective-permute-start(bf16[32,80,128]{2,1,0:T(8,128)(2,1)S(1)} %all_gather.7.refs_3_), channel_id=1, source_target_pairs={{0,8},{1,25},{2,10},{3,27},{4,12},{5,29},{6,14},{7,31},{8,0},{9,17... | collective-permute-start | bytes 1966088 | tf_op jit(solution)/shard_map/gather_amplitudes/ppermute | solution.py:229

commit v5 on v4

--- a/solution.py
+++ b/solution.py
@@ -225,11 +225,13 @@
     with jax.named_scope("route_tiles"):
         own_tiles = lax.all_to_all(outgoing, G, 0, 0, tiled=True)
     with jax.named_scope("gather_amplitudes"):
-        gathered = lax.all_gather(lax.all_gather(share, "zh", axis=0, tiled=True), "zl", axis=0, tiled=True)
+        gathered = lax.all_gather(share, "zh", axis=0, tiled=True)
+        own_tiles, gathered = lax.optimization_barrier((own_tiles, gathered))
+        gathered = jnp.broadcast_to(gathered, (ZL, *gathered.shape))
+        gathered = lax.all_to_all(gathered, "zl", 0, 0, tiled=True).reshape(ZL * ZH, size, TILE)
         both, along_x, along_y = (lax.ppermute(gathered, G, step(d)) for d in ORDER[:3])
         pieces = [both, along_x, along_y, gathered]
     with jax.named_scope("share_tiles"):
-        own_tiles, _ = lax.optimization_barrier((own_tiles, gathered))
         far_tiles = lax.ppermute(own_tiles, "core", [(0, 1), (1, 0)])
         own_label, far_label = (t[:, CAP * TILE, :CAP].astype(jnp.int32) for t in (own_tiles, far_tiles))
     with jax.named_scope("product"):

time: 162 us -> 159 us (0.981)
  blocking collectives: 115 us -> 96.4 us
  waiting for transfers between devices: 7.12 us -> 16.5 us
  starting transfers between devices: 28 us -> 31.5 us
    all_gather x2 -> x1, blocking collectives: 60 us -> 43.3 us  [on_device(): gathered = lax.all_gather(share, 'zh', axis=0, tiled=True)]
    all_to_all x0 -> x1, waiting for transfers between devices: none -> 10.8 us  [on_device(): lax.all_to_all(gathered, 'zl', 0, 0, tiled=True)]
    all_to_all x0 -> x1, starting transfers between devices: none -> 3.48 us  [on_device(): lax.all_to_all(gathered, 'zl', 0, 0, tiled=True)]
    all_to_all x1, blocking collectives: 17.3 us -> 15.1 us  [on_device(): near = lax.all_to_all(partial, ('zl', 'core'), 0, 0, tiled=True)]
  transfers between devices with their start and end apart: 5 -> 6, of which waited for: 3 -> 3; matrix products, arithmetic and copies ran while one was open for 0% -> 1% of each run, Pallas kernels for 2% -> 3%
where the time goes in v5:
time: 159 us; the launch traced here: 158 us
  blocking collectives  96.4 us (61%)
  starting transfers between devices  31.5 us (20%)
  waiting for transfers between devices  16.5 us (10%)
  Pallas kernels  10.5 us (7%)
  other arithmetic  1.91 us (1%)
    all_gather x1, blocking collectives, on_device(): gathered = lax.all_gather(share, 'zh', axis=0, tiled=True)  43.3 us
    all_to_all x1, blocking collectives, on_device(): return far_sum(lax.all_to_all(near, 'zh', 0, 0, tiled=True), rows)  38.1 us
    all_to_all x1, starting transfers between devices, on_device(): own_tiles = lax.all_to_all(outgoing, G, 0, 0, tiled=True)  16.8 us
    all_to_all x1, blocking collectives, on_device(): near = lax.all_to_all(partial, ('zl', 'core'), 0, 0, tiled=True)  15.1 us
    all_to_all x1, waiting for transfers between devices, on_device(): lax.all_to_all(gathered, 'zl', 0, 0, tiled=True)  10.8 us
    ppermute x3, starting transfers between devices, on_device(): lax.ppermute(gathered, G, step(d))  9.2 us
    ppermute x3, waiting for transfers between devices, on_device(): lax.ppermute(gathered, G, step(d))  5.71 us
    pallas_call x1, Pallas kernels, cells(): pl.pallas_call(cells_kernel, out_shape=jax.ShapeDtypeStruct((n_cd, TILE,...  4.47 us
  transfers between devices with their start and end apart: 6, of which 3 were waited for; matrix products, arithmetic and copies ran while one was open for 1% of the time, Pallas kernels for 3%

profile of v5, /device:TPU:6, one launch (start us, length us, event | category | flops | bytes accessed | tf_op | source)
XLA Modules:
  0.0 158.1 jit_solution(6685687568874173809)
XLA Ops:
  0.0 0.0 copy-start
  0.0 3.8 %pack.1 = bf16[32,272,128]{2,1,0:T(8,128)(2,1)} custom-call(s32[32]{0:T(128)} %cd_ref.1, s32[32]{0:T(128)} %ab_ref.1, s32[64]{0:T(128)} %owner_ref.1, bf16[32,128,128]{2,1,0:T(8,128)(2,1)} %tiles_ref.1), custom_call_target="tpu_custom_call" | custom-call | bytes 3145728 | tf_op jit(solution)/shard_map/pack/pack/pallas_call | solution.py:76
  3.8 16.8 %all-to-all-start = ((bf16[32,272,128]{2,1,0:T(8,128)(2,1)}), bf16[32,272,128]{2,1,0:T(8,128)(2,1)S(1)}, u32[]{:S(2)}, u32[]{:S(2)}) async-start(bf16[32,272,128]{2,1,0:T(8,128)(2,1)} %pack.1), calls=%async_computation | async-start | bytes 4456448 | tf_op jit(solution)/shard_map/route_tiles/all_to_all | solution.py:226
  20.6 0.0 copy-done
  20.7 43.3 %all_gather.3 = bf16[8,80,128]{2,1,0:T(8,128)(2,1)S(1)} all-gather(bf16[1,80,128]{2,1,0:T(8,128)(2,1)S(1)} %constant_dynamic-slice_fusion), channel_id=1, replica_groups=mesh['zh'=8,'zl'=4,'y'=4,'x'=4,'core'=2] {'zh'}, dimensions={0}, use_global_device_ids=true | all-gather | bytes 184320 | tf_op jit(solution)/shard_map/gather_amplitudes/all_gather | solution.py:228
  63.9 0.0 all-to-all-done.own_tiles
  64.0 0.9 broadcast_in_dim.14
  64.9 3.5 %all-to-all-start.1 = ((bf16[4,8,80,128]{3,2,1,0:T(8,128)(2,1)}), bf16[4,8,80,128]{3,2,1,0:T(8,128)(2,1)S(1)}, u32[]{:S(2)}, u32[]{:S(2)}) async-start(bf16[4,8,80,128]{3,2,1,0:T(8,128)(2,1)} %broadcast_in_dim.14), calls=%async_computation.1 | async-start | bytes 1310720 | tf_op jit(solution)/shard_map/gather_amplitudes/all_to_all | solution.py:231
  68.4 1.9 %collective-permute-start.3 = (bf16[32,272,128]{2,1,0:T(8,128)(2,1)S(1)}, bf16[32,272,128]{2,1,0:T(8,128)(2,1)}, u32[]{:S(2)}, u32[]{:S(2)}) collective-permute-start(bf16[32,272,128]{2,1,0:T(8,128)(2,1)S(1)} %all-to-all-done.own_tiles), channel_id=1, source_target_pairs={{0,1},{1,0},{2,3},{3,2},{4,5},{5,4},{6,7},{7,6},{8,9},{9,8},{10,11... | collective-permute-start | bytes 6684680 | tf_op jit(solution)/shard_map/share_tiles/ppermute | solution.py:235
  70.3 10.8 %all-to-all-done.1 = bf16[4,8,80,128]{3,2,1,0:T(8,128)(2,1)S(1)} async-done(((bf16[4,8,80,128]{3,2,1,0:T(8,128)(2,1)}), bf16[4,8,80,128]{3,2,1,0:T(8,128)(2,1)S(1)}, u32[]{:S(2)}, u32[]{:S(2)}) %all-to-all-start.1) | async-done | bytes 655392 | tf_op jit(solution)/shard_map/gather_amplitudes/all_to_all | solution.py:231
  81.1 2.7 %collective-permute-start = (bf16[32,80,128]{2,1,0:T(8,128)(2,1)S(1)}, bf16[32,80,128]{2,1,0:T(8,128)(2,1)S(1)}, u32[]{:S(2)}, u32[]{:S(2)}) collective-permute-start(bf16[32,80,128]{2,1,0:T(8,128)(2,1)S(1)} %bitcast.14), channel_id=1, source_target_pairs={{0,10},{1,31},{2,8},{3,29},{4,14},{5,27},{6,12},{7,25},{8,2},{9,23... | collective-permute-start | bytes 1966088 | tf_op jit(solution)/shard_map/gather_amplitudes/ppermute | solution.py:232
  83.8 3.2 %collective-permute-start.1 = (bf16[32,80,128]{2,1,0:T(8,128)(2,1)S(1)}, bf16[32,80,128]{2,1,0:T(8,128)(2,1)S(1)}, u32[]{:S(2)}, u32[]{:S(2)}) collective-permute-start(bf16[32,80,128]{2,1,0:T(8,128)(2,1)S(1)} %bitcast.15), channel_id=1, source_target_pairs={{0,2},{1,7},{2,0},{3,5},{4,6},{5,3},{6,4},{7,1},{8,10},{9,15},{10,... | collective-permute-start | bytes 1966088 | tf_op jit(solution)/shard_map/gather_amplitudes/ppermute | solution.py:232
  87.0 3.3 %collective-permute-start.2 = (bf16[32,80,128]{2,1,0:T(8,128)(2,1)S(1)}, bf16[32,80,128]{2,1,0:T(8,128)(2,1)S(1)}, u32[]{:S(2)}, u32[]{:S(2)}) collective-permute-start(bf16[32,80,128]{2,1,0:T(8,128)(2,1)S(1)} %bitcast.16), channel_id=1, source_target_pairs={{0,8},{1,25},{2,10},{3,27},{4,12},{5,29},{6,14},{7,31},{8,0},{9,17... | collective-permute-start | bytes 1966088 | tf_op jit(solution)/shard_map/gather_amplitudes/ppermute | solution.py:232
  90.3 0.1 pad_add_fusion.place_ref
  90.4 0.0 collective-permute-done.3.far_tiles
  90.4 0.9 slice_convert_fusion
  91.3 4.5 %cells.1.refs_4_ = bf16[32,128,512]{2,1,0:T(8,128)(2,1)S(1)} custom-call(s32[32,2]{1,0:T(8,128)S(1)} %bitcast.18, s32[32,2]{1,0:T(8,128)S(1)} %bitcast.19, bf16[32,272,128]{2,1,0:T(8,128)(2,1)S(1)} %all-to-all-done.own_tiles, bf16[32,272,128]{2,1,0:T(8,128)(2,1)} %collective-permute-done.3.far_tiles), custom_call_target="tpu_custom_call" | custom-call | bytes 12582912 | tf_op jit(solution)/shard_map/product/cells/pallas_call | solution.py:113
  95.8 0.0 collective-permute-done.refs_0_
  95.8 4.9 %collective-permute-done.1.refs_1_ = bf16[32,80,128]{2,1,0:T(8,128)(2,1)S(1)} collective-permute-done((bf16[32,80,128]{2,1,0:T(8,128)(2,1)S(1)}, bf16[32,80,128]{2,1,0:T(8,128)(2,1)S(1)}, u32[]{:S(2)}, u32[]{:S(2)}) %collective-permute-start.1) | collective-permute-done | bytes 655392 | tf_op jit(solution)/shard_map/gather_amplitudes/ppermute | solution.py:232
  100.7 0.8 collective-permute-done.2.refs_2_
  101.5 2.3 %product.1 = s16[8,96,256]{2,1,0:T(8,128)(2,1)S(1)} custom-call(s32[2]{0:T(128)S(1)} %pad_add_fusion.place_ref, bf16[32,80,128]{2,1,0:T(8,128)(2,1)S(1)} %collective-permute-done.refs_0_, bf16[32,80,128]{2,1,0:T(8,128)(2,1)S(1)} %collective-permute-done.1.refs_1_, bf16[32,80,128]{2,1,0:T(8,128)(2,1)S(1)} %collective-permute-done.2.refs_2_, ...), custom_call_target="tpu_custom_call" | custom-call | flops 1342177280 | bytes 8388608 | tf_op jit(solution)/shard_map/product/product/pallas_call | solution.py:164
  103.8 15.1 %all_to_all.20 = s16[8,96,256]{2,1,0:T(8,128)(2,1)S(1)} all-to-all(s16[8,96,256]{2,1,0:T(8,128)(2,1)S(1)} %product.1), channel_id=1, replica_groups=mesh['zh'=8,'zl'=4,'y'=4,'x'=4,'core'=2] {'zl','core'}, dimensions={0} | all-to-all | bytes 786432 | tf_op jit(solution)/shard_map/reduce/all_to_all | solution.py:241
  118.9 0.1 bitcast_convert_fusion
  119.0 0.1 fusion
  119.3 38.1 %all_to_all.21 = s16[8,24,256]{2,1,0:T(8,128)(2,1)S(1)} all-to-all(s16[8,24,256]{2,1,0:T(8,128)(2,1)S(1)} %fusion.2), channel_id=1, replica_groups=mesh['zh'=8,'zl'=4,'y'=4,'x'=4,'core'=2] {'zh'}, dimensions={0} | all-to-all | bytes 196608 | tf_op jit(solution)/shard_map/reduce/all_to_all | solution.py:243
  157.4 0.6 fusion.1
  (17 shorter events, 0.3 us)
Async XLA Ops:
  0.0 20.6 %copy-start = (bf16[1,640,128]{2,1,0:T(8,128)(2,1)S(1)}, bf16[1,640,128]{2,1,0:T(8,128)(2,1)}, u32[]{:S(2)}) copy-start(bf16[1,640,128]{2,1,0:T(8,128)(2,1)} %param.5) | copy-start | bytes 491524
  3.8 60.2 %all-to-all-start = ((bf16[32,272,128]{2,1,0:T(8,128)(2,1)}), bf16[32,272,128]{2,1,0:T(8,128)(2,1)S(1)}, u32[]{:S(2)}, u32[]{:S(2)}) async-start(bf16[32,272,128]{2,1,0:T(8,128)(2,1)} %pack.1), calls=%async_computation | async-start | bytes 4456448 | tf_op jit(solution)/shard_map/route_tiles/all_to_all | solution.py:226
  64.9 16.2 %all-to-all-start.1 = ((bf16[4,8,80,128]{3,2,1,0:T(8,128)(2,1)}), bf16[4,8,80,128]{3,2,1,0:T(8,128)(2,1)S(1)}, u32[]{:S(2)}, u32[]{:S(2)}) async-start(bf16[4,8,80,128]{3,2,1,0:T(8,128)(2,1)} %broadcast_in_dim.14), calls=%async_computation.1 | async-start | bytes 1310720 | tf_op jit(solution)/shard_map/gather_amplitudes/all_to_all | solution.py:231
  68.4 22.0 %collective-permute-start.3 = (bf16[32,272,128]{2,1,0:T(8,128)(2,1)S(1)}, bf16[32,272,128]{2,1,0:T(8,128)(2,1)}, u32[]{:S(2)}, u32[]{:S(2)}) collective-permute-start(bf16[32,272,128]{2,1,0:T(8,128)(2,1)S(1)} %all-to-all-done.own_tiles), channel_id=1, source_target_pairs={{0,1},{1,0},{2,3},{3,2},{4,5},{5,4},{6,7},{7,6},{8,9},{9,8},{10,11... | collective-permute-start | bytes 6684680 | tf_op jit(solution)/shard_map/share_tiles/ppermute | solution.py:235
  81.1 14.7 %collective-permute-start = (bf16[32,80,128]{2,1,0:T(8,128)(2,1)S(1)}, bf16[32,80,128]{2,1,0:T(8,128)(2,1)S(1)}, u32[]{:S(2)}, u32[]{:S(2)}) collective-permute-start(bf16[32,80,128]{2,1,0:T(8,128)(2,1)S(1)} %bitcast.14), channel_id=1, source_target_pairs={{0,10},{1,31},{2,8},{3,29},{4,14},{5,27},{6,12},{7,25},{8,2},{9,23... | collective-permute-start | bytes 1966088 | tf_op jit(solution)/shard_map/gather_amplitudes/ppermute | solution.py:232
  83.8 16.8 %collective-permute-start.1 = (bf16[32,80,128]{2,1,0:T(8,128)(2,1)S(1)}, bf16[32,80,128]{2,1,0:T(8,128)(2,1)S(1)}, u32[]{:S(2)}, u32[]{:S(2)}) collective-permute-start(bf16[32,80,128]{2,1,0:T(8,128)(2,1)S(1)} %bitcast.15), channel_id=1, source_target_pairs={{0,2},{1,7},{2,0},{3,5},{4,6},{5,3},{6,4},{7,1},{8,10},{9,15},{10,... | collective-permute-start | bytes 1966088 | tf_op jit(solution)/shard_map/gather_amplitudes/ppermute | solution.py:232
  87.0 14.5 %collective-permute-start.2 = (bf16[32,80,128]{2,1,0:T(8,128)(2,1)S(1)}, bf16[32,80,128]{2,1,0:T(8,128)(2,1)S(1)}, u32[]{:S(2)}, u32[]{:S(2)}) collective-permute-start(bf16[32,80,128]{2,1,0:T(8,128)(2,1)S(1)} %bitcast.16), channel_id=1, source_target_pairs={{0,8},{1,25},{2,10},{3,27},{4,12},{5,29},{6,14},{7,31},{8,0},{9,17... | collective-permute-start | bytes 1966088 | tf_op jit(solution)/shard_map/gather_amplitudes/ppermute | solution.py:232

commit v6 on v5

--- a/solution.py
+++ b/solution.py
@@ -24,11 +24,15 @@
 
 
 def pack_kernel(
-    cd_ref, ab_ref, owner_ref, tiles_ref, out_ref, count_ref, label_ref, task_ref, held, message, in_sem, out_sems
+    cd_ref, ab_ref, owner_ref, tiles_ref, out_ref, count_ref, label_ref, slot_ref, held, label_rows, in_sems, out_sems, label_sem
 ):
-    tasks, groups, parts = tiles_ref.shape[0], out_ref.shape[0], out_sems.shape[0]
-    fetch = pltpu.make_async_copy(tiles_ref, held, in_sem)
-    fetch.start()
+    tasks, groups, parts = tiles_ref.shape[0], out_ref.shape[0], in_sems.shape[0]
+    size = tasks // parts
+    fetches = []
+    for part in range(parts):
+        some = pl.ds(part * size, size)
+        fetches.append(pltpu.make_async_copy(tiles_ref.at[some], held.at[some], in_sems.at[part]))
+        fetches[-1].start()
 
     @pl.loop(0, groups)
     def _(g):
@@ -45,30 +49,35 @@
         cd = cd_ref[k]
         cell = (cd & (ZL - 1)) * ZH + (cd >> 2)
         label_ref[CAP * group + arrival] = 2 * cell + (position & 1)
-        task_ref[CAP * group + arrival] = k
-
-    fetch.wait()
+        slot_ref[k] = CAP * group + arrival
+
     lane = lax.broadcasted_iota(jnp.int32, (LABEL_ROWS, TILE), 1)
-    size = groups // parts
-    sends = []
-    for part in range(parts):
+
+    @pl.loop(0, groups)
+    def _(g):
+        labels = jnp.where(lane == 0, label_ref[CAP * g], label_ref[CAP * g + 1])
+        label_rows[g] = labels.astype(jnp.float32).astype(label_rows.dtype)
+
+    label_send = pltpu.make_async_copy(label_rows, out_ref.at[:, pl.ds(CAP * TILE, LABEL_ROWS), :], label_sem)
+    label_send.start()
+
+    def send(k):
+        slot = slot_ref[k]
+        row = pl.multiple_of((slot & (CAP - 1)) * TILE, TILE)
+        return pltpu.make_async_copy(held.at[k], out_ref.at[slot >> 1, pl.ds(row, TILE), :], out_sems.at[k])
+
+    for part, fetch in enumerate(fetches):
+        fetch.wait()
 
         @pl.loop(part * size, (part + 1) * size)
-        def _(g):
-            for n in range(CAP):
-
-                @pl.when(label_ref[CAP * g + n] >= 0)
-                def _():
-                    message[g, n * TILE : (n + 1) * TILE, :] = held[task_ref[CAP * g + n]]
-
-            labels = jnp.where(lane == 0, label_ref[CAP * g], label_ref[CAP * g + 1])
-            message[g, CAP * TILE :, :] = labels.astype(jnp.float32).astype(message.dtype)
-
-        group = pl.ds(part * size, size)
-        sends.append(pltpu.make_async_copy(message.at[group], out_ref.at[group], out_sems.at[part]))
-        sends[-1].start()
-    for send in sends:
-        send.wait()
+        def _(k):
+            send(k).start()
+
+    @pl.loop(0, tasks)
+    def _(k):
+        send(k).wait()
+
+    label_send.wait()
 
 
 def pack(task_cd, task_ab, owner_map, tiles, groups):
@@ -81,11 +90,12 @@
         scratch_shapes=[
             pltpu.SMEM((groups,), jnp.int32),
             pltpu.SMEM((groups * CAP,), jnp.int32),
-            pltpu.SMEM((groups * CAP,), jnp.int32),
+            pltpu.SMEM((tiles.shape[0],), jnp.int32),
             pltpu.VMEM(tiles.shape, tiles.dtype),
-            pltpu.VMEM(out, tiles.dtype),
+            pltpu.VMEM((groups, LABEL_ROWS, TILE), tiles.dtype),
+            pltpu.SemaphoreType.DMA((4,)),
+            pltpu.SemaphoreType.DMA((tiles.shape[0],)),
             pltpu.SemaphoreType.DMA,
-            pltpu.SemaphoreType.DMA((4,)),
         ],
         compiler_params=pltpu.CompilerParams(vmem_limit_bytes=56 * MIB),
         cost_estimate=pl.CostEstimate(flops=0, bytes_accessed=3 * MIB, transcendentals=0),

time: 159 us -> 158 us (level)
  no operation moved by 1% of the time
where the time goes in v6:
time: 158 us; the launch traced here: 157 us
  blocking collectives  96.3 us (61%)
  starting transfers between devices  31.5 us (20%)
  waiting for transfers between devices  16.5 us (10%)
  Pallas kernels  9.87 us (6%)
  other arithmetic  1.91 us (1%)
    all_gather x1, blocking collectives, on_device(): gathered = lax.all_gather(share, 'zh', axis=0, tiled=True)  43.2 us
    all_to_all x1, blocking collectives, on_device(): return far_sum(lax.all_to_all(near, 'zh', 0, 0, tiled=True), rows)  38 us
    all_to_all x1, starting transfers between devices, on_device(): own_tiles = lax.all_to_all(outgoing, G, 0, 0, tiled=True)  16.9 us
    all_to_all x1, blocking collectives, on_device(): near = lax.all_to_all(partial, ('zl', 'core'), 0, 0, tiled=True)  15.1 us
    all_to_all x1, waiting for transfers between devices, on_device(): lax.all_to_all(gathered, 'zl', 0, 0, tiled=True)  10.8 us
    ppermute x3, starting transfers between devices, on_device(): lax.ppermute(gathered, G, step(d))  9.2 us
    ppermute x3, waiting for transfers between devices, on_device(): lax.ppermute(gathered, G, step(d))  5.71 us
    pallas_call x1, Pallas kernels, cells(): pl.pallas_call(cells_kernel, out_shape=jax.ShapeDtypeStruct((n_cd, TILE,...  4.47 us
  transfers between devices with their start and end apart: 6, of which 3 were waited for; matrix products, arithmetic and copies ran while one was open for 1% of the time, Pallas kernels for 3%

profile of v6, /device:TPU:6, one launch (start us, length us, event | category | flops | bytes accessed | tf_op | source)
XLA Modules:
  0.0 157.3 jit_solution(1398694137971588223)
XLA Ops:
  0.0 0.0 copy-start
  0.0 3.1 %pack.1 = bf16[32,272,128]{2,1,0:T(8,128)(2,1)} custom-call(s32[32]{0:T(128)} %cd_ref.1, s32[32]{0:T(128)} %ab_ref.1, s32[64]{0:T(128)} %owner_ref.1, bf16[32,128,128]{2,1,0:T(8,128)(2,1)} %tiles_ref.1), custom_call_target="tpu_custom_call" | custom-call | bytes 3145728 | tf_op jit(solution)/shard_map/pack/pack/pallas_call | solution.py:85
  3.1 16.9 %all-to-all-start = ((bf16[32,272,128]{2,1,0:T(8,128)(2,1)}), bf16[32,272,128]{2,1,0:T(8,128)(2,1)S(1)}, u32[]{:S(2)}, u32[]{:S(2)}) async-start(bf16[32,272,128]{2,1,0:T(8,128)(2,1)} %pack.1), calls=%async_computation | async-start | bytes 4456448 | tf_op jit(solution)/shard_map/route_tiles/all_to_all | solution.py:236
  20.0 0.0 copy-done
  20.0 43.2 %all_gather.3 = bf16[8,80,128]{2,1,0:T(8,128)(2,1)S(1)} all-gather(bf16[1,80,128]{2,1,0:T(8,128)(2,1)S(1)} %constant_dynamic-slice_fusion), channel_id=1, replica_groups=mesh['zh'=8,'zl'=4,'y'=4,'x'=4,'core'=2] {'zh'}, dimensions={0}, use_global_device_ids=true | all-gather | bytes 184320 | tf_op jit(solution)/shard_map/gather_amplitudes/all_gather | solution.py:238
  63.2 0.0 all-to-all-done.own_tiles
  63.2 0.9 broadcast_in_dim.14
  64.2 3.5 %all-to-all-start.1 = ((bf16[4,8,80,128]{3,2,1,0:T(8,128)(2,1)}), bf16[4,8,80,128]{3,2,1,0:T(8,128)(2,1)S(1)}, u32[]{:S(2)}, u32[]{:S(2)}) async-start(bf16[4,8,80,128]{3,2,1,0:T(8,128)(2,1)} %broadcast_in_dim.14), calls=%async_computation.1 | async-start | bytes 1310720 | tf_op jit(solution)/shard_map/gather_amplitudes/all_to_all | solution.py:241
  67.6 1.9 %collective-permute-start.3 = (bf16[32,272,128]{2,1,0:T(8,128)(2,1)S(1)}, bf16[32,272,128]{2,1,0:T(8,128)(2,1)}, u32[]{:S(2)}, u32[]{:S(2)}) collective-permute-start(bf16[32,272,128]{2,1,0:T(8,128)(2,1)S(1)} %all-to-all-done.own_tiles), channel_id=1, source_target_pairs={{0,1},{1,0},{2,3},{3,2},{4,5},{5,4},{6,7},{7,6},{8,9},{9,8},{10,11... | collective-permute-start | bytes 6684680 | tf_op jit(solution)/shard_map/share_tiles/ppermute | solution.py:245
  69.6 10.8 %all-to-all-done.1 = bf16[4,8,80,128]{3,2,1,0:T(8,128)(2,1)S(1)} async-done(((bf16[4,8,80,128]{3,2,1,0:T(8,128)(2,1)}), bf16[4,8,80,128]{3,2,1,0:T(8,128)(2,1)S(1)}, u32[]{:S(2)}, u32[]{:S(2)}) %all-to-all-start.1) | async-done | bytes 655392 | tf_op jit(solution)/shard_map/gather_amplitudes/all_to_all | solution.py:241
  80.4 2.8 %collective-permute-start = (bf16[32,80,128]{2,1,0:T(8,128)(2,1)S(1)}, bf16[32,80,128]{2,1,0:T(8,128)(2,1)S(1)}, u32[]{:S(2)}, u32[]{:S(2)}) collective-permute-start(bf16[32,80,128]{2,1,0:T(8,128)(2,1)S(1)} %bitcast.14), channel_id=1, source_target_pairs={{0,10},{1,31},{2,8},{3,29},{4,14},{5,27},{6,12},{7,25},{8,2},{9,23... | collective-permute-start | bytes 1966088 | tf_op jit(solution)/shard_map/gather_amplitudes/ppermute | solution.py:242
  83.2 3.1 %collective-permute-start.1 = (bf16[32,80,128]{2,1,0:T(8,128)(2,1)S(1)}, bf16[32,80,128]{2,1,0:T(8,128)(2,1)S(1)}, u32[]{:S(2)}, u32[]{:S(2)}) collective-permute-start(bf16[32,80,128]{2,1,0:T(8,128)(2,1)S(1)} %bitcast.15), channel_id=1, source_target_pairs={{0,2},{1,7},{2,0},{3,5},{4,6},{5,3},{6,4},{7,1},{8,10},{9,15},{10,... | collective-permute-start | bytes 1966088 | tf_op jit(solution)/shard_map/gather_amplitudes/ppermute | solution.py:242
  86.3 3.3 %collective-permute-start.2 = (bf16[32,80,128]{2,1,0:T(8,128)(2,1)S(1)}, bf16[32,80,128]{2,1,0:T(8,128)(2,1)S(1)}, u32[]{:S(2)}, u32[]{:S(2)}) collective-permute-start(bf16[32,80,128]{2,1,0:T(8,128)(2,1)S(1)} %bitcast.16), channel_id=1, source_target_pairs={{0,8},{1,25},{2,10},{3,27},{4,12},{5,29},{6,14},{7,31},{8,0},{9,17... | collective-permute-start | bytes 1966088 | tf_op jit(solution)/shard_map/gather_amplitudes/ppermute | solution.py:242
  89.6 0.1 pad_add_fusion.place_ref
  89.7 0.0 collective-permute-done.3.far_tiles
  89.7 0.9 slice_convert_fusion
  90.6 4.5 %cells.1.refs_4_ = bf16[32,128,512]{2,1,0:T(8,128)(2,1)S(1)} custom-call(s32[32,2]{1,0:T(8,128)S(1)} %bitcast.18, s32[32,2]{1,0:T(8,128)S(1)} %bitcast.19, bf16[32,272,128]{2,1,0:T(8,128)(2,1)S(1)} %all-to-all-done.own_tiles, bf16[32,272,128]{2,1,0:T(8,128)(2,1)} %collective-permute-done.3.far_tiles), custom_call_target="tpu_custom_call" | custom-call | bytes 12582912 | tf_op jit(solution)/shard_map/product/cells/pallas_call | solution.py:123
  95.0 0.0 collective-permute-done.refs_0_
  95.1 4.9 %collective-permute-done.1.refs_1_ = bf16[32,80,128]{2,1,0:T(8,128)(2,1)S(1)} collective-permute-done((bf16[32,80,128]{2,1,0:T(8,128)(2,1)S(1)}, bf16[32,80,128]{2,1,0:T(8,128)(2,1)S(1)}, u32[]{:S(2)}, u32[]{:S(2)}) %collective-permute-start.1) | collective-permute-done | bytes 655392 | tf_op jit(solution)/shard_map/gather_amplitudes/ppermute | solution.py:242
  100.0 0.8 collective-permute-done.2.refs_2_
  100.8 2.3 %product.1 = s16[8,96,256]{2,1,0:T(8,128)(2,1)S(1)} custom-call(s32[2]{0:T(128)S(1)} %pad_add_fusion.place_ref, bf16[32,80,128]{2,1,0:T(8,128)(2,1)S(1)} %collective-permute-done.refs_0_, bf16[32,80,128]{2,1,0:T(8,128)(2,1)S(1)} %collective-permute-done.1.refs_1_, bf16[32,80,128]{2,1,0:T(8,128)(2,1)S(1)} %collective-permute-done.2.refs_2_, ...), custom_call_target="tpu_custom_call" | custom-call | flops 1342177280 | bytes 8388608 | tf_op jit(solution)/shard_map/product/product/pallas_call | solution.py:174
  103.0 15.1 %all_to_all.20 = s16[8,96,256]{2,1,0:T(8,128)(2,1)S(1)} all-to-all(s16[8,96,256]{2,1,0:T(8,128)(2,1)S(1)} %product.1), channel_id=1, replica_groups=mesh['zh'=8,'zl'=4,'y'=4,'x'=4,'core'=2] {'zl','core'}, dimensions={0} | all-to-all | bytes 786432 | tf_op jit(solution)/shard_map/reduce/all_to_all | solution.py:251
  118.1 0.1 bitcast_convert_fusion
  118.3 0.1 fusion
  118.6 38.0 %all_to_all.21 = s16[8,24,256]{2,1,0:T(8,128)(2,1)S(1)} all-to-all(s16[8,24,256]{2,1,0:T(8,128)(2,1)S(1)} %fusion.2), channel_id=1, replica_groups=mesh['zh'=8,'zl'=4,'y'=4,'x'=4,'core'=2] {'zh'}, dimensions={0} | all-to-all | bytes 196608 | tf_op jit(solution)/shard_map/reduce/all_to_all | solution.py:253
  156.7 0.6 fusion.1
  (17 shorter events, 0.3 us)
Async XLA Ops:
  0.0 20.0 %copy-start = (bf16[1,640,128]{2,1,0:T(8,128)(2,1)S(1)}, bf16[1,640,128]{2,1,0:T(8,128)(2,1)}, u32[]{:S(2)}) copy-start(bf16[1,640,128]{2,1,0:T(8,128)(2,1)} %param.5) | copy-start | bytes 491524
  3.1 60.1 %all-to-all-start = ((bf16[32,272,128]{2,1,0:T(8,128)(2,1)}), bf16[32,272,128]{2,1,0:T(8,128)(2,1)S(1)}, u32[]{:S(2)}, u32[]{:S(2)}) async-start(bf16[32,272,128]{2,1,0:T(8,128)(2,1)} %pack.1), calls=%async_computation | async-start | bytes 4456448 | tf_op jit(solution)/shard_map/route_tiles/all_to_all | solution.py:236
  64.2 16.2 %all-to-all-start.1 = ((bf16[4,8,80,128]{3,2,1,0:T(8,128)(2,1)}), bf16[4,8,80,128]{3,2,1,0:T(8,128)(2,1)S(1)}, u32[]{:S(2)}, u32[]{:S(2)}) async-start(bf16[4,8,80,128]{3,2,1,0:T(8,128)(2,1)} %broadcast_in_dim.14), calls=%async_computation.1 | async-start | bytes 1310720 | tf_op jit(solution)/shard_map/gather_amplitudes/all_to_all | solution.py:241
  67.6 22.1 %collective-permute-start.3 = (bf16[32,272,128]{2,1,0:T(8,128)(2,1)S(1)}, bf16[32,272,128]{2,1,0:T(8,128)(2,1)}, u32[]{:S(2)}, u32[]{:S(2)}) collective-permute-start(bf16[32,272,128]{2,1,0:T(8,128)(2,1)S(1)} %all-to-all-done.own_tiles), channel_id=1, source_target_pairs={{0,1},{1,0},{2,3},{3,2},{4,5},{5,4},{6,7},{7,6},{8,9},{9,8},{10,11... | collective-permute-start | bytes 6684680 | tf_op jit(solution)/shard_map/share_tiles/ppermute | solution.py:245
  80.4 14.7 %collective-permute-start = (bf16[32,80,128]{2,1,0:T(8,128)(2,1)S(1)}, bf16[32,80,128]{2,1,0:T(8,128)(2,1)S(1)}, u32[]{:S(2)}, u32[]{:S(2)}) collective-permute-start(bf16[32,80,128]{2,1,0:T(8,128)(2,1)S(1)} %bitcast.14), channel_id=1, source_target_pairs={{0,10},{1,31},{2,8},{3,29},{4,14},{5,27},{6,12},{7,25},{8,2},{9,23... | collective-permute-start | bytes 1966088 | tf_op jit(solution)/shard_map/gather_amplitudes/ppermute | solution.py:242
  83.2 16.8 %collective-permute-start.1 = (bf16[32,80,128]{2,1,0:T(8,128)(2,1)S(1)}, bf16[32,80,128]{2,1,0:T(8,128)(2,1)S(1)}, u32[]{:S(2)}, u32[]{:S(2)}) collective-permute-start(bf16[32,80,128]{2,1,0:T(8,128)(2,1)S(1)} %bitcast.15), channel_id=1, source_target_pairs={{0,2},{1,7},{2,0},{3,5},{4,6},{5,3},{6,4},{7,1},{8,10},{9,15},{10,... | collective-permute-start | bytes 1966088 | tf_op jit(solution)/shard_map/gather_amplitudes/ppermute | solution.py:242
  86.3 14.4 %collective-permute-start.2 = (bf16[32,80,128]{2,1,0:T(8,128)(2,1)S(1)}, bf16[32,80,128]{2,1,0:T(8,128)(2,1)S(1)}, u32[]{:S(2)}, u32[]{:S(2)}) collective-permute-start(bf16[32,80,128]{2,1,0:T(8,128)(2,1)S(1)} %bitcast.16), channel_id=1, source_target_pairs={{0,8},{1,25},{2,10},{3,27},{4,12},{5,29},{6,14},{7,31},{8,0},{9,17... | collective-permute-start | bytes 1966088 | tf_op jit(solution)/shard_map/gather_amplitudes/ppermute | solution.py:242
